TPU v7x, 512 devices: a whole 4x4x16 slice. The times are simulated.
512 devices in a mesh: cell: 64 (over z, y), mode: 8 (over x, core).
Axes of the slice: x: 4, y: 4, z: 16, core: 2. Of those that a mesh axis runs over, the one named last changes fastest.
Arguments:
- source: bfloat16 [2048, 64, 1024], P('mode', 'cell'), may hold values from -6 to 6
- prior: bfloat16 [2048, 64, 1024], P('mode', 'cell'), may hold values from -6 to 6
- coupling: bfloat16 [16, 4, 128, 128], P('mode'), may hold values from -0.25 to 0.25
- pairs: int32 [16, 4], replicated, may hold values from 0 to 15, all different within a row
- transmission: float32 [3, 2048], P(None, 'mode'), may hold values from 0 to 1, as said below
- direction: int32 [3, 2048], P(None, 'mode'), may hold values from 0 to 1
Outputs:
- distribution: bfloat16 [2048, 64, 1024], P('mode', 'cell')
Inputs may be any that keep to these rules, and one draw needn't show every extreme that they name: Each row of pairs names 4 different column blocks, and every column block is named by some row. `transmission`: each entry lies strictly between 0 and 1.
All inputs are finite; a program needn't handle non-finite values.
Results may differ from a plain program's by a relative error of at most 0.0023.
Values may be sent and summed in bfloat16 or wider, within the bound.
A program may use at most 64 MiB of HBM per device.

v0:
```python
import jax
import jax.numpy as jnp
from jax import lax
from jax.sharding import PartitionSpec as P

ITERS = 2
NY = 32
NZ = 32


def block_product(values, blocks, chosen):
    row_count, per_row, width = (blocks.shape[0], blocks.shape[1], blocks.shape[2])
    flat_rows = values.reshape(values.shape[0] // width, width, values.shape[1] * values.shape[2])
    picked = jnp.take(flat_rows, chosen, axis=0)
    right_side = picked.reshape(row_count, per_row * width, values.shape[1] * values.shape[2])
    left_side = blocks.transpose(0, 2, 1, 3).reshape(row_count, width, per_row * width)
    product = jnp.einsum("rab,rbc->rac", left_side, right_side, preferred_element_type=jnp.float32)
    return product.reshape(row_count * width, values.shape[1], values.shape[2])


def sweep_matrix(decay_rate, forward, length):
    positions = jnp.arange(length, dtype=jnp.int32)
    lag_steps = positions[:, None] - positions[None, :]
    lag_steps = jnp.where(forward[:, None, None] == 1, lag_steps[None], -lag_steps[None])
    power = jnp.exp(
        jnp.maximum(lag_steps, 0).astype(jnp.float32) * jnp.log(decay_rate)[:, None, None]
    )
    weight = jnp.sqrt(1.0 - decay_rate * decay_rate)[:, None, None]
    return jnp.where(lag_steps >= 0, weight * power, 0.0)


def stream(volume, decays, senses):
    modes, length, plane_cells = volume.shape
    along_x = sweep_matrix(decays[0], senses[0], length)
    volume = jnp.einsum("mij,mjp->mip", along_x, volume, precision=lax.Precision.HIGHEST)
    cube_view = volume.reshape(modes, length, NY, NZ)
    along_y = sweep_matrix(decays[1], senses[1], NY)
    cube_view = jnp.einsum("mij,mxjz->mxiz", along_y, cube_view, precision=lax.Precision.HIGHEST)
    along_z = sweep_matrix(decays[2], senses[2], NZ)
    cube_view = jnp.einsum("mij,mxyj->mxyi", along_z, cube_view, precision=lax.Precision.HIGHEST)
    return cube_view.reshape(modes, length, plane_cells)


def local(source, prior, coupling, pairs, transmission, direction):
    cells_axis = lax.axis_size("cell")
    local_modes = source.shape[0]
    per_device = local_modes // cells_axis
    offset = lax.axis_index("cell") * per_device
    decays = lax.dynamic_slice_in_dim(transmission, offset, per_device, 1)
    senses = lax.dynamic_slice_in_dim(direction, offset, per_device, 1)
    emission = source.astype(jnp.float32)
    current = prior
    coupling_all = lax.all_gather(coupling, "mode", axis=0, tiled=True)
    for iteration in range(ITERS):
        spread = lax.all_to_all(current, "mode", split_axis=2, concat_axis=0, tiled=True)
        mixed_rows = block_product(spread, coupling_all, pairs)
        scattered = lax.all_to_all(mixed_rows, "mode", split_axis=0, concat_axis=2, tiled=True)
        regrouped = lax.all_to_all(
            emission + scattered, "cell", split_axis=0, concat_axis=1, tiled=True
        )
        swept_rows = stream(regrouped, decays, senses).astype(jnp.bfloat16)
        current = lax.all_to_all(swept_rows, "cell", split_axis=1, concat_axis=0, tiled=True)
    return current


def solution(mesh):
    in_specs = (
        P("mode", "cell", None),
        P("mode", "cell", None),
        P("mode", None, None, None),
        P(),
        P(None, "mode"),
        P(None, "mode"),
    )
    out_specs = P("mode", "cell", None)
    return jax.shard_map(local, mesh=mesh, in_specs=in_specs, out_specs=out_specs, check_vma=False)
```

profile of v0, /device:TPU:8, one launch (start us, length us, event | category | flops | bytes accessed | tf_op | source)
XLA Modules:
  0.0 349.7 jit_solution(723715658645579438)
XLA Ops:
  6.5 0.7 all-gather.2.cloned.1.call-update
  7.3 2.4 copy.54
  10.3 4.0 %reduce = bf16[1024,256]{1,0:T(8,128)(2,1)S(1)} reduce(bf16[1024,1,256]{2,1,0:T(2,128)(2,1)S(1)} %bitcast.124, bf16[]{:T(256)} %broadcast.110), dimensions={1}, to_apply=%bitcast.97.reduce_sub_computation | reduce | bytes 1048578
  14.2 0.9 reshape.202
  15.2 4.3 %all-to-all-start = ((bf16[8,2,16384]{2,1,0:T(2,128)(2,1)}), bf16[8,2,16384]{2,1,0:T(2,128)(2,1)S(1)}, u32[]{:S(2)}, u32[]{:S(2)}) async-start(bf16[8,2,16384]{2,1,0:T(2,128)(2,1)} %reshape.202), calls=%async_computation | async-start | bytes 1048576 | tf_op jit(solution)/shard_map/all_to_all | solution.py:55
  19.8 10.0 %all-to-all-done = bf16[8,2,16384]{2,1,0:T(2,128)(2,1)S(1)} async-done(((bf16[8,2,16384]{2,1,0:T(2,128)(2,1)}), bf16[8,2,16384]{2,1,0:T(2,128)(2,1)S(1)}, u32[]{:S(2)}, u32[]{:S(2)}) %all-to-all-start) | async-done | bytes 524320 | tf_op jit(solution)/shard_map/all_to_all | solution.py:55
  30.7 2.1 gather_fusion
  32.9 1.8 broadcast_select_fusion
  34.7 12.0 %all-gather.2.cloned.1.call-done = bf16[16,4,128,128]{3,2,1,0:T(8,128)(2,1)} async-done(((bf16[2,4,128,128]{3,2,1,0:T(8,128)(2,1)}), bf16[16,4,128,128]{3,2,1,0:T(8,128)(2,1)}) %all-gather.2.cloned.1.call-update) | async-done | bytes 2097168 | tf_op jit(solution)/shard_map/all_gather | solution.py:53
  46.7 2.4 fusion
  49.1 19.3 %all_to_all.138 = f32[2048,1,128]{2,1,0:T(1,128)S(1)} all-to-all(f32[2048,1,128]{2,1,0:T(1,128)S(1)} %bitcast.118), channel_id=1, replica_groups=mesh['cell'=64,'mode'=8] {'mode'}, dimensions={0} | all-to-all | bytes 2097152 | tf_op jit(solution)/shard_map/all_to_all | solution.py:57
  69.1 2.1 fusion.33
  71.2 16.3 %all-to-all-start.2 = ((f32[256,1,1024]{2,1,0:T(1,128)}), f32[256,1,1024]{2,1,0:T(1,128)S(1)}, u32[]{:S(2)}, u32[]{:S(2)}) async-start(f32[256,1,1024]{2,1,0:T(1,128)} %fusion.33), calls=%async_computation.2 | async-start | bytes 2097152 | tf_op jit(solution)/shard_map/all_to_all | solution.py:58
  87.7 54.5 %all-to-all-done.2 = f32[256,1,1024]{2,1,0:T(1,128)S(1)} async-done(((f32[256,1,1024]{2,1,0:T(1,128)}), f32[256,1,1024]{2,1,0:T(1,128)S(1)}, u32[]{:S(2)}, u32[]{:S(2)}) %all-to-all-start.2) | async-done | bytes 1048608 | tf_op jit(solution)/shard_map/all_to_all | solution.py:58
  142.2 3.7 %fusion.28 = f32[4,64,1024]{1,2,0:T(8,128)S(1)} fusion(f32[64,4,1,1024]{3,2,1,0:T(1,128)S(1)} %bitcast.121, f32[4]{0:T(128)S(1)} %get-tuple-element.10, f32[4]{0:T(128)S(1)} %get-tuple-element.14, s32[64,64]{1,0:T(8,128)S(1)} %get-tuple-element.16, s32[64,64]{1,0:T(8,128)S(1)} %get-tuple-element.15, pred[4]{0:T(512)(128)(4,1)S(1)} %get-tuple-element.8), kind=kOutput, calls=%fused_computation.24 | convolution fusion | flops 201441280 | bytes 2129956 | tf_op jit(solution)/shard_map/mij,mjp->mip/dot_general | solution.py:35
  145.9 3.2 fusion.14
  149.1 3.2 fusion.20
  153.0 37.5 %all_to_all.139 = bf16[4,64,1024]{2,0,1:T(4,128)(2,1)S(1)} all-to-all(bf16[4,64,1024]{2,0,1:T(4,128)(2,1)S(1)} %copy.64), channel_id=1, replica_groups=mesh['cell'=64,'mode'=8] {'cell'}, dimensions={1} | all-to-all | bytes 1048576 | tf_op jit(solution)/shard_map/all_to_all | solution.py:62
  190.6 0.9 copy.65
  191.5 4.0 %reduce.1 = bf16[1024,256]{1,0:T(8,128)(2,1)S(1)} reduce(bf16[1024,1,256]{2,1,0:T(2,128)(2,1)S(1)} %bitcast.125, bf16[]{:T(256)} %broadcast.110), dimensions={1}, to_apply=%bitcast.99.reduce_sub_computation | reduce | bytes 1048578
  195.6 12.8 %all_to_all.140 = bf16[8,2,16384]{2,1,0:T(2,128)(2,1)S(1)} all-to-all(bf16[8,2,16384]{2,1,0:T(2,128)(2,1)S(1)} %reshape.204), channel_id=1, replica_groups=mesh['cell'=64,'mode'=8] {'mode'}, dimensions={0} | all-to-all | bytes 1048576 | tf_op jit(solution)/shard_map/all_to_all | solution.py:55
  209.3 1.0 gather_fusion.1
  210.6 1.3 copy-done.1
  211.9 0.7 fusion.2
  212.6 18.5 %all_to_all.141 = f32[2048,1,128]{2,1,0:T(1,128)S(1)} all-to-all(f32[2048,1,128]{2,1,0:T(1,128)S(1)} %bitcast.117), channel_id=1, replica_groups=mesh['cell'=64,'mode'=8] {'mode'}, dimensions={0} | all-to-all | bytes 2097152 | tf_op jit(solution)/shard_map/all_to_all | solution.py:57
  231.7 1.1 fusion.32
  232.8 60.8 %all_to_all.142 = f32[256,1,1024]{2,1,0:T(1,128)S(1)} all-to-all(f32[256,1,1024]{2,1,0:T(1,128)S(1)} %fusion.32), channel_id=1, replica_groups=mesh['cell'=64,'mode'=8] {'cell'}, dimensions={0} | all-to-all | bytes 2097152 | tf_op jit(solution)/shard_map/all_to_all | solution.py:58
  293.6 3.7 %fusion.26 = f32[4,64,1024]{1,2,0:T(8,128)S(1)} fusion(f32[64,4,1,1024]{3,2,1,0:T(1,128)S(1)} %bitcast.122, f32[4]{0:T(128)S(1)} %get-tuple-element.10, f32[4]{0:T(128)S(1)} %get-tuple-element.14, s32[64,64]{1,0:T(8,128)S(1)} %get-tuple-element.16, s32[64,64]{1,0:T(8,128)S(1)} %get-tuple-element.15, pred[4]{0:T(512)(128)(4,1)S(1)} %get-tuple-element.8), kind=kOutput, calls=%fused_computation.22 | convolution fusion | flops 201441280 | bytes 2129956 | tf_op jit(solution)/shard_map/mij,mjp->mip/dot_general | solution.py:35
  297.3 3.2 fusion.17
  300.5 3.2 fusion.23
  304.4 37.3 %all_to_all.143 = bf16[4,64,1024]{2,0,1:T(4,128)(2,1)S(1)} all-to-all(bf16[4,64,1024]{2,0,1:T(4,128)(2,1)S(1)} %copy.74), channel_id=1, replica_groups=mesh['cell'=64,'mode'=8] {'cell'}, dimensions={1} | all-to-all | bytes 1048576 | tf_op jit(solution)/shard_map/all_to_all | solution.py:62
  341.7 0.9 all_to_all.129
  (36 shorter events, 5.9 us)
Async XLA Ops:
  6.5 81.0 %copy-start = (f32[3,256]{1,0:T(4,128)S(1)}, f32[3,256]{1,0:T(4,128)}, u32[]{:S(2)}) copy-start(f32[3,256]{1,0:T(4,128)} %param.12) | copy-start | bytes 9220
  6.5 40.2 %all-gather.2.cloned.1.call-start = ((), (), s32[]{:S(2)}) async-start(), calls=%async_computation.8 | async-start | bytes 2359296 | tf_op jit(solution)/shard_map/all_gather | solution.py:53
  9.7 9.8 %copy-start.3 = (s32[16,4]{0,1:T(4,128)S(1)}, s32[16,4]{0,1:T(4,128)}, u32[]{:S(2)}) copy-start(s32[16,4]{0,1:T(4,128)} %param.11) | copy-start | bytes 772
  15.2 14.6 %all-to-all-start = ((bf16[8,2,16384]{2,1,0:T(2,128)(2,1)}), bf16[8,2,16384]{2,1,0:T(2,128)(2,1)S(1)}, u32[]{:S(2)}, u32[]{:S(2)}) async-start(bf16[8,2,16384]{2,1,0:T(2,128)(2,1)} %reshape.202), calls=%async_computation | async-start | bytes 1048576 | tf_op jit(solution)/shard_map/all_to_all | solution.py:55
  49.1 20.0 %copy-start.2 = (bf16[256,1,1024]{2,0,1:T(8,128)(2,1)S(1)}, bf16[256,1,1024]{2,0,1:T(8,128)(2,1)}, u32[]{:S(2)}) copy-start(bf16[256,1,1024]{2,0,1:T(8,128)(2,1)} %param.8) | copy-start | bytes 1572868
  69.1 18.5 %copy-start.4 = (s32[3,256]{1,0:T(4,128)S(1)}, s32[3,256]{1,0:T(4,128)}, u32[]{:S(2)}) copy-start(s32[3,256]{1,0:T(4,128)} %param.13) | copy-start | bytes 9220
  71.2 71.0 %all-to-all-start.2 = ((f32[256,1,1024]{2,1,0:T(1,128)}), f32[256,1,1024]{2,1,0:T(1,128)S(1)}, u32[]{:S(2)}, u32[]{:S(2)}) async-start(f32[256,1,1024]{2,1,0:T(1,128)} %fusion.33), calls=%async_computation.2 | async-start | bytes 2097152 | tf_op jit(solution)/shard_map/all_to_all | solution.py:58
  210.3 1.6 copy-start.1
Sparse Core Ops, SparseCore 0:
  9.5 37.1 all-gather.1
where the time goes:
time: 357 us; the launch traced here: 350 us
  blocking collectives  186 us (52%)
  waiting for transfers between devices  77.2 us (22%)
  matrix products  23.4 us (7%)
  starting transfers between devices  20.6 us (6%)
  local copies, waits for them, and re-layouts  15 us (4%)
  between operations  13.9 us (4%)
  other arithmetic  13.3 us (4%)
    all_to_all x2, blocking collectives, local(): lax.all_to_all(swept_rows, 'cell', split_axis=1, concat_axis=0, tiled=True)  74.8 us
    all_to_all x1, blocking collectives, local(): lax.all_to_all(emission + scattered, 'cell', split_axis=0, concat_axis=1,...  60.8 us
    all_to_all x1, waiting for transfers between devices, local(): lax.all_to_all(emission + scattered, 'cell', split_axis=0, concat_axis=1,...  54.5 us
    all_to_all x2, blocking collectives, local(): lax.all_to_all(mixed_rows, 'mode', split_axis=0, concat_axis=2, tiled=True)  37.9 us
    all_to_all x1, starting transfers between devices, local(): lax.all_to_all(emission + scattered, 'cell', split_axis=0, concat_axis=1,...  16.3 us
    all_to_all x1, blocking collectives, local(): lax.all_to_all(current, 'mode', split_axis=2, concat_axis=0, tiled=True)  12.8 us
    all_gather x1, waiting for transfers between devices, local(): coupling_all = lax.all_gather(coupling, 'mode', axis=0, tiled=True)  12 us
    all_to_all x1, waiting for transfers between devices, local(): lax.all_to_all(current, 'mode', split_axis=2, concat_axis=0, tiled=True)  10 us
  transfers between devices with their start and end apart: 3, of which 3 were waited for; matrix products, arithmetic and copies ran while one was open for 4% of the time, Pallas kernels for 0%

commit v1 on v0

v1 whole, which is shorter than its diff:
```python
import functools

import jax
import jax.numpy as jnp
from jax import lax
from jax.experimental import pallas as pl
from jax.experimental.pallas import tpu as pltpu
from jax.sharding import PartitionSpec as P

ITERS = 2
BLOCK = 128
PER_ROW = 4
ZLO = 8
YLO = 4
XLO = 4
TOP = 32767.0
F32 = jnp.float32
BF16 = jnp.bfloat16
I16 = jnp.int16
MESH = pl.DeviceIdType.MESH


def nt(left, right):
    return lax.dot_general(left, right, (((1,), (1,)), ((), ())), preferred_element_type=F32)


def identity(size):
    rows = lax.broadcasted_iota(jnp.int32, (size, size), 0)
    columns = lax.broadcasted_iota(jnp.int32, (size, size), 1)
    return jnp.where(rows == columns, 1.0, 0.0).astype(BF16)


def run(values, factor, forward):
    n = len(values)
    ordered = [jnp.where(forward, values[s], values[n - 1 - s]) for s in range(n)]
    swept = [ordered[0]]
    for s in range(1, n):
        swept.append(factor * swept[-1] + ordered[s])
    return [jnp.where(forward, swept[s], swept[n - 1 - s]) for s in range(n)]


def encode(values, scale):
    return jnp.round(values * scale).astype(jnp.int32).astype(I16)


def decode(codes):
    return codes.astype(jnp.int32).astype(F32)


def kernel(
    dims,
    source,
    prior,
    coupling,
    pairs,
    transmission,
    direction,
    out,
    cur_a,
    cur_b,
    emission,
    turned,
    turned_s,
    blocks,
    coef_own,
    coef,
    work,
    x_send,
    x_recv,
    xs_send,
    xs_recv,
    planes,
    ends,
    e_send,
    e_recv,
    es_send,
    es_recv,
    b_send,
    b_recv,
    bs_send,
    bs_recv,
    c_send,
    f_send,
    f_recv,
    s0_send,
    s0_recv,
    gather_send,
    gather_recv,
    x_sem,
    e_sem,
    b_sem,
    c_sem,
    f_sem,
    scale_sem,
):
    nm, ny_dev, nz_dev, ny, nz = dims
    chips = nm // 2
    chunk = YLO * nz
    tall = ny * ZLO
    per_z = tall // nz_dev
    me_m = lax.axis_index("mode")
    me_c = lax.axis_index("cell")
    me_z, me_y = me_c // ny_dev, me_c % ny_dev
    me_x, me_core = me_m // 2, me_m % 2

    def remote(src, dst, send, recv, to):
        return pltpu.make_async_remote_copy(
            src_ref=src, dst_ref=dst, send_sem=send, recv_sem=recv, device_id=to, device_id_type=MESH
        )

    def await_bytes(ref, sem):
        pltpu.make_async_copy(ref, ref, sem).wait()

    barrier = pltpu.get_barrier_semaphore()
    group = nm * ny_dev

    def greet_group(j, carry):
        m = (me_m + j // ny_dev) % nm
        y = (me_y + j % ny_dev) % ny_dev
        pl.semaphore_signal(barrier, inc=1, device_id=(me_z * ny_dev + y, m), device_id_type=MESH)
        return carry

    lax.fori_loop(1, group, greet_group, 0)

    def greet_ring(j, carry):
        z = (me_z + j) % nz_dev
        pl.semaphore_signal(barrier, inc=1, device_id=(z * ny_dev + me_y, me_m), device_id_type=MESH)
        return carry

    lax.fori_loop(1, nz_dev, greet_ring, 0)

    fwd = {}
    fac = {}
    weight = {}
    for h in range(2):
        lanes = slice(h * BLOCK, (h + 1) * BLOCK)
        for d in range(3):
            fac[d, h] = jnp.broadcast_to(transmission[d : d + 1, lanes], (8, BLOCK))
            fwd[d, h] = jnp.broadcast_to(direction[d : d + 1, lanes], (8, BLOCK)) == 1
        total = jnp.sqrt(1.0 - transmission[0:1, lanes] * transmission[0:1, lanes])
        for d in range(1, 3):
            total = total * jnp.sqrt(1.0 - transmission[d : d + 1, lanes] * transmission[d : d + 1, lanes])
        weight[h] = total
    for h in range(2):
        coef_own[0, h * 4 : h * 4 + 4, :] = fac[2, h][:4]
        coef_own[1, h * 4 : h * 4 + 4, :] = jnp.where(fwd[2, h], 1.0, 0.0)[:4]

    eye = identity(chunk)

    def turn(array, into):
        for m in range(nm):
            for h in range(2):
                tile = nt(eye, array[h * BLOCK : (h + 1) * BLOCK, m * chunk : (m + 1) * chunk])
                rows = [
                    tile[y * nz + zh * ZLO : y * nz + (zh + 1) * ZLO]
                    for zh in range(ny_dev)
                    for y in range(YLO)
                ]
                into[m, h] = jnp.concatenate(rows, axis=0).astype(BF16)

    turn(prior, turned)
    pl.semaphore_wait(barrier, group - 1 + nz_dev - 1)

    local = pltpu.make_async_copy(turned.at[me_m], cur_a.at[me_m], s0_recv.at[0])
    local.start()
    for j in range(1, nm):
        m = (me_m + j) % nm
        remote(turned.at[m], cur_a.at[me_m], s0_send.at[0], s0_recv.at[0], (me_c, m)).start()
    pltpu.make_async_copy(coef_own, coef.at[me_m], s0_recv.at[2]).start()
    for j in range(1, nm):
        m = (me_m + j) % nm
        remote(coef_own, coef.at[me_m], s0_send.at[2], s0_recv.at[2], (me_c, m)).start()
    sibling = me_x * 2 + 1 - me_core
    for j in range(1, chips):
        x = (me_x + j) % chips
        remote(
            coupling, blocks.at[me_m], gather_send.at[0], gather_recv.at[j], (me_c, x * 2 + me_core)
        ).start()
    remote(coupling, blocks.at[me_m], gather_send.at[1], gather_recv.at[0], (me_c, sibling)).start()
    own_blocks = pltpu.make_async_copy(coupling, blocks.at[me_m], gather_send.at[3])
    own_blocks.start()
    turn(source, turned_s)
    pltpu.make_async_copy(turned_s.at[me_m], emission.at[me_m], s0_recv.at[1]).start()
    for j in range(1, nm):
        m = (me_m + j) % nm
        remote(turned_s.at[m], emission.at[me_m], s0_send.at[1], s0_recv.at[1], (me_c, m)).start()
    for j in range(1, chips):
        m = ((me_x + chips - j) % chips) * 2 + me_core
        await_bytes(blocks.at[m], gather_recv.at[j])
        remote(blocks.at[m], blocks.at[m], gather_send.at[2], gather_recv.at[0], (me_c, sibling)).start()
    own_blocks.wait()
    await_bytes(cur_a, s0_recv.at[0])
    await_bytes(coef, s0_recv.at[2])
    await_bytes(blocks.at[pl.ds(0, chips)], gather_recv.at[0])
    await_bytes(emission, s0_recv.at[1])

    for iteration in range(ITERS):
        current = cur_a if iteration == 0 else cur_b
        last = iteration == ITERS - 1

        def scatter(j, carry):
            m = (me_m + 1 + j) % nm
            for h in range(2):
                row = m * 2 + h
                left = jnp.concatenate([current[pairs[row, k] // 2, pairs[row, k] % 2] for k in range(PER_ROW)], axis=1)
                right = jnp.concatenate([blocks[m, h * PER_ROW + k] for k in range(PER_ROW)], axis=1)
                total = nt(left, right) + emission[m, h].astype(F32)
                for zh in range(ny_dev):
                    for y in range(YLO):
                        work[h * chunk + y * nz + zh * ZLO : h * chunk + y * nz + (zh + 1) * ZLO, :] = total[
                            (zh * YLO + y) * ZLO : (zh * YLO + y + 1) * ZLO
                        ]
            values = [work[pl.ds(z, 8, stride=nz), :] for z in range(nz)]
            values = run(values, coef[m, 0], coef[m, 1] > 0.5)
            largest = jnp.abs(values[0])
            for z in range(nz):
                work[pl.ds(z, 8, stride=nz), :] = values[z]
                if z:
                    largest = jnp.maximum(largest, jnp.abs(values[z]))
            largest = jnp.maximum(jnp.max(largest, axis=0, keepdims=True), 1e-30)
            xs_send[m] = largest * (1.0 / TOP)
            scale = TOP / largest
            for zh in range(ny_dev):
                for h in range(2):
                    for y in range(0, YLO, 2):
                        rows = [
                            work[h * chunk + (y + i) * nz + zh * ZLO : h * chunk + (y + i) * nz + (zh + 1) * ZLO, :]
                            for i in range(2)
                        ]
                        x_send[m * ny_dev + zh, h, y * ZLO : (y + 2) * ZLO, :] = encode(
                            jnp.concatenate(rows, axis=0), scale
                        )
            slot = me_m * ny_dev + me_y
            for i in range(ny_dev):
                y = (me_y + 1 + i) % ny_dev
                to = (me_z * ny_dev + y, m)

                def send():
                    remote(x_send.at[m * ny_dev + y], x_recv.at[slot], x_sem.at[0], x_sem.at[1], to).start()
                    remote(xs_send.at[m], xs_recv.at[slot], scale_sem.at[0], scale_sem.at[1], to).start()

                def keep():
                    pltpu.make_async_copy(x_send.at[m * ny_dev + y], x_recv.at[slot], x_sem.at[1]).start()
                    pltpu.make_async_copy(xs_send.at[m], xs_recv.at[slot], scale_sem.at[1]).start()

                if i < ny_dev - 1:
                    send()
                else:
                    pl.when(j < nm - 1)(send)
                    pl.when(j == nm - 1)(keep)
            return carry

        lax.fori_loop(0, nm, scatter, 0)
        await_bytes(x_recv, x_sem.at[1])
        await_bytes(xs_recv, scale_sem.at[1])

        def unpack(m, carry):
            for h in range(2):
                got = []
                for x in range(XLO):
                    factor = xs_recv[m * ny_dev + x] * weight[h]
                    value = decode(x_recv[m * ny_dev + x, h]) * factor
                    planes[h, x, pl.ds(m * YLO * ZLO, YLO * ZLO), :] = value
                    got.append(value)
                t = jnp.concatenate([fac[0, h]] * YLO, axis=0)
                f = jnp.concatenate([transmission_dir(h)] * YLO, axis=0) == 1
                end = jnp.where(f, got[0], got[XLO - 1])
                for x in range(1, XLO):
                    end = end * t + jnp.where(f, got[x], got[XLO - 1 - x])
                ends[h, pl.ds(m * YLO * ZLO, YLO * ZLO), :] = end
            return carry

        def transmission_dir(h):
            return jnp.broadcast_to(direction[0:1, h * BLOCK : (h + 1) * BLOCK], (8, BLOCK))

        lax.fori_loop(0, nm, unpack, 0)
        largest = jnp.full((8, BLOCK), 1e-30, F32)
        for h in range(2):
            values = [ends[h, y * ZLO : (y + 1) * ZLO, :] for y in range(ny)]
            values = run(values, fac[1, h], fwd[1, h])
            for y in range(ny):
                ends[h, y * ZLO : (y + 1) * ZLO, :] = values[y]
                largest = jnp.maximum(largest, jnp.abs(values[y]))
        largest = jnp.max(largest, axis=0, keepdims=True)
        es_send[...] = largest * (1.0 / TOP)
        scale = TOP / largest

        def send_ends(j, carry):
            z = (me_z + 1 + j) % nz_dev
            for h in range(2):
                e_send[z, h] = encode(ends[h, pl.ds(z * per_z, per_z), :], scale)
            to = (z * ny_dev + me_y, me_m)

            @pl.when(j < nz_dev - 1)
            def _():
                remote(e_send.at[z], e_recv.at[me_z], e_sem.at[0], e_sem.at[1], to).start()
                remote(es_send, es_recv.at[me_z], scale_sem.at[2], scale_sem.at[3], to).start()

            @pl.when(j == nz_dev - 1)
            def _():
                pltpu.make_async_copy(e_send.at[z], e_recv.at[me_z], e_sem.at[1]).start()
                pltpu.make_async_copy(es_send, es_recv.at[me_z], scale_sem.at[3]).start()

            return carry

        lax.fori_loop(0, nz_dev, send_ends, 0)

        def sweep_y(h):
            def one(x, carry):
                values = [planes[h, x, y * ZLO : (y + 1) * ZLO, :] for y in range(ny)]
                values = run(values, fac[1, h], fwd[1, h])
                for y in range(ny):
                    planes[h, x, y * ZLO : (y + 1) * ZLO, :] = values[y]
                return carry

            lax.fori_loop(0, XLO, one, 0)

        sweep_y(0)
        await_bytes(e_recv, e_sem.at[1])
        await_bytes(es_recv, scale_sem.at[3])

        largest = jnp.full((8, BLOCK), 1e-30, F32)
        for h in range(2):
            leap = fac[0, h] * fac[0, h]
            leap = leap * leap
            for part in range(per_z // 16):
                got = [
                    decode(e_recv[z, h, part * 16 : part * 16 + 16, :]) * es_recv[z] for z in range(nz_dev)
                ]
                for i in range(2):
                    f = fwd[0, h]
                    given = [g[i * 8 : i * 8 + 8] for g in got]
                    ordered = [jnp.where(f, given[s], given[nz_dev - 1 - s]) for s in range(nz_dev)]
                    taken = [jnp.zeros_like(ordered[0])]
                    for s in range(nz_dev - 1):
                        taken.append(leap * taken[-1] + ordered[s])
                    for z in range(nz_dev):
                        value = jnp.where(f, taken[z], taken[nz_dev - 1 - z])
                        ends[h, z * per_z + part * 16 + i * 8 : z * per_z + part * 16 + i * 8 + 8, :] = value
                        largest = jnp.maximum(largest, jnp.abs(value))
        largest = jnp.max(largest, axis=0, keepdims=True)
        bs_send[...] = largest * (1.0 / TOP)
        scale = TOP / largest

        def send_back(j, carry):
            z = (me_z + 1 + j) % nz_dev
            for h in range(2):
                b_send[z, h] = encode(ends[h, pl.ds(z * per_z, per_z), :], scale)
            to = (z * ny_dev + me_y, me_m)

            @pl.when(j < nz_dev - 1)
            def _():
                remote(b_send.at[z], b_recv.at[me_z], b_sem.at[0], b_sem.at[1], to).start()
                remote(bs_send, bs_recv.at[me_z], scale_sem.at[4], scale_sem.at[5], to).start()

            @pl.when(j == nz_dev - 1)
            def _():
                pltpu.make_async_copy(b_send.at[z], b_recv.at[me_z], b_sem.at[1]).start()
                pltpu.make_async_copy(bs_send, bs_recv.at[me_z], scale_sem.at[5]).start()

            return carry

        lax.fori_loop(0, nz_dev, send_back, 0)
        sweep_y(1)
        await_bytes(b_recv, b_sem.at[1])
        await_bytes(bs_recv, scale_sem.at[5])

        def inflow(z, carry):
            for h in range(2):
                ends[h, pl.ds(z * per_z, per_z), :] = decode(b_recv[z, h]) * bs_recv[z]
            return carry

        lax.fori_loop(0, nz_dev, inflow, 0)

        def finish(j, carry):
            m = (me_m + 1 + j) % nm
            rows = pl.ds(m * YLO * ZLO, YLO * ZLO)
            for h in range(2):
                t = jnp.concatenate([fac[0, h]] * YLO, axis=0)
                f = jnp.concatenate([transmission_dir(h)] * YLO, axis=0) == 1
                given = [planes[h, x, rows, :] for x in range(XLO)]
                value = ends[h, rows, :]
                swept = []
                for x in range(XLO):
                    value = t * value + jnp.where(f, given[x], given[XLO - 1 - x])
                    swept.append(value)
                for x in range(XLO):
                    result = jnp.where(f, swept[x], swept[XLO - 1 - x]).astype(BF16)
                    if last:
                        f_send[x, h, rows, :] = result
                    else:
                        c_send[m * ny_dev + x, h] = result
            if not last:
                for i in range(ny_dev):
                    y = (me_y + 1 + i) % ny_dev
                    to = (me_z * ny_dev + y, m)
                    into = cur_b.at[me_m, :, pl.ds(me_y * YLO * ZLO, YLO * ZLO), :]

                    def send():
                        remote(c_send.at[m * ny_dev + y], into, c_sem.at[0], c_sem.at[1], to).start()

                    def keep():
                        pltpu.make_async_copy(c_send.at[m * ny_dev + y], into, c_sem.at[1]).start()

                    if i < ny_dev - 1:
                        send()
                    else:
                        pl.when(j < nm - 1)(send)
                        pl.when(j == nm - 1)(keep)
            return carry

        lax.fori_loop(0, nm, finish, 0)
        await_bytes(x_send.at[pl.ds(0, group - 1)], x_sem.at[0])
        await_bytes(xs_recv.at[pl.ds(0, group - 1)], scale_sem.at[0])
        await_bytes(e_send.at[pl.ds(0, nz_dev - 1)], e_sem.at[0])
        await_bytes(es_recv.at[pl.ds(0, nz_dev - 1)], scale_sem.at[2])
        await_bytes(b_send.at[pl.ds(0, nz_dev - 1)], b_sem.at[0])
        await_bytes(bs_recv.at[pl.ds(0, nz_dev - 1)], scale_sem.at[4])
        if not last:
            await_bytes(cur_b, c_sem.at[1])
            await_bytes(c_send.at[pl.ds(0, group - 1)], c_sem.at[0])

    for i in range(1, ny_dev):
        y = (me_y + i) % ny_dev
        remote(f_send.at[y], f_recv.at[me_y], f_sem.at[0], f_sem.at[1], (me_z * ny_dev + y, me_m)).start()
    pltpu.make_async_copy(f_send.at[me_y], f_recv.at[me_y], f_sem.at[1]).start()
    await_bytes(turned.at[pl.ds(0, nm - 1)], s0_send.at[0])
    await_bytes(turned_s.at[pl.ds(0, nm - 1)], s0_send.at[1])
    await_bytes(coef.at[pl.ds(0, nm - 1)], s0_send.at[2])
    if chips > 1:
        await_bytes(blocks.at[pl.ds(0, chips - 1)], gather_send.at[0])
        await_bytes(blocks.at[pl.ds(0, chips - 1)], gather_send.at[2])
    await_bytes(coupling, gather_send.at[1])
    await_bytes(f_recv, f_sem.at[1])
    wide = identity(BLOCK)
    for m in range(nm):
        for h in range(2):
            parts = []
            for zh in range(ny_dev):
                parts.append(f_recv[zh, h, m * YLO * ZLO : (m + 1) * YLO * ZLO, :].astype(F32))
            rows = [parts[zh][y * ZLO : (y + 1) * ZLO] for y in range(YLO) for zh in range(ny_dev)]
            tile = jnp.concatenate(rows, axis=0).astype(BF16)
            out[h * BLOCK : (h + 1) * BLOCK, m * chunk : (m + 1) * chunk] = nt(wide, tile).astype(BF16)
    await_bytes(f_send.at[pl.ds(0, ny_dev - 1)], f_sem.at[0])


def local(dims, source, prior, coupling, pairs, transmission, direction):
    nm, ny_dev, nz_dev, ny, nz = dims
    modes = source.shape[0]
    group = nm * ny_dev
    chunk = YLO * nz
    tall = ny * ZLO
    per_z = tall // nz_dev
    vmem = pl.BlockSpec(memory_space=pltpu.VMEM)
    dma = pltpu.SemaphoreType.DMA
    result = pl.pallas_call(
        functools.partial(kernel, dims),
        out_shape=jax.ShapeDtypeStruct((modes, ny * nz), BF16),
        in_specs=[vmem, vmem, vmem, pl.BlockSpec(memory_space=pltpu.SMEM), vmem, vmem],
        out_specs=vmem,
        scratch_shapes=[
            pltpu.VMEM((nm, 2, chunk, BLOCK), BF16),
            pltpu.VMEM((nm, 2, chunk, BLOCK), BF16),
            pltpu.VMEM((nm, 2, chunk, BLOCK), BF16),
            pltpu.VMEM((nm, 2, chunk, BLOCK), BF16),
            pltpu.VMEM((nm, 2, chunk, BLOCK), BF16),
            pltpu.VMEM((nm, 2 * PER_ROW, BLOCK, BLOCK), BF16),
            pltpu.VMEM((2, 8, BLOCK), F32),
            pltpu.VMEM((nm, 2, 8, BLOCK), F32),
            pltpu.VMEM((2 * chunk, BLOCK), F32),
            pltpu.VMEM((group, 2, YLO * ZLO, BLOCK), I16),
            pltpu.VMEM((group, 2, YLO * ZLO, BLOCK), I16),
            pltpu.VMEM((nm, 1, BLOCK), F32),
            pltpu.VMEM((group, 1, BLOCK), F32),
            pltpu.VMEM((2, XLO, tall, BLOCK), F32),
            pltpu.VMEM((2, tall, BLOCK), F32),
            pltpu.VMEM((nz_dev, 2, per_z, BLOCK), I16),
            pltpu.VMEM((nz_dev, 2, per_z, BLOCK), I16),
            pltpu.VMEM((1, BLOCK), F32),
            pltpu.VMEM((nz_dev, 1, BLOCK), F32),
            pltpu.VMEM((nz_dev, 2, per_z, BLOCK), I16),
            pltpu.VMEM((nz_dev, 2, per_z, BLOCK), I16),
            pltpu.VMEM((1, BLOCK), F32),
            pltpu.VMEM((nz_dev, 1, BLOCK), F32),
            pltpu.VMEM((group, 2, YLO * ZLO, BLOCK), BF16),
            pltpu.VMEM((ny_dev, 2, tall, BLOCK), BF16),
            pltpu.VMEM((ny_dev, 2, tall, BLOCK), BF16),
            dma((3,)),
            dma((3,)),
            dma((4,)),
            dma((nm // 2,)),
            dma((2,)),
            dma((2,)),
            dma((2,)),
            dma((2,)),
            dma((2,)),
            dma((6,)),
        ],
        compiler_params=pltpu.CompilerParams(
            collective_id=0, has_side_effects=True, vmem_limit_bytes=40 * 1024 * 1024
        ),
        cost_estimate=pl.CostEstimate(flops=600_000_000, bytes_accessed=2_000_000, transcendentals=0),
    )(
        source.reshape(modes, ny * nz),
        prior.reshape(modes, ny * nz),
        coupling.reshape(2 * PER_ROW, BLOCK, BLOCK),
        pairs,
        transmission,
        direction,
    )
    return result.reshape(modes, 1, ny * nz)


def build(mesh, ny, nz):
    nm = mesh.shape["mode"]
    ny_dev = nz // ZLO
    nz_dev = mesh.shape["cell"] // ny_dev
    in_specs = (
        P("mode", "cell", None),
        P("mode", "cell", None),
        P("mode", None, None, None),
        P(),
        P(None, "mode"),
        P(None, "mode"),
    )
    body = functools.partial(local, (nm, ny_dev, nz_dev, ny, nz))
    return jax.shard_map(body, mesh=mesh, in_specs=in_specs, out_specs=P("mode", "cell", None), check_vma=False)


def solution(mesh):
    return build(mesh, 32, 32)
```

time: 357 us -> 129 us (0.36)
  the two profiles are of different devices: /device:TPU:8 before, /device:TPU:6 now
where the time goes in v1:
time: 129 us; the launch traced here: 128 us
  Pallas kernels  123 us (95%)
  local copies, waits for them, and re-layouts  5.21 us (4%)
    pallas_call x1, Pallas kernels, local(): pl.pallas_call(functools.partial(kernel, dims), out_shape=jax.ShapeDtypeS...  123 us
    unnamed x14, local copies, waits for them, and re-layouts  5.21 us

profile of v1, /device:TPU:6, one launch (start us, length us, event | category | flops | bytes accessed | tf_op | source)
XLA Modules:
  0.0 128.3 jit_solution(9817842347994588451)
XLA Ops:
  0.0 0.0 copy-start.5
  0.0 0.7 copy-done.5
  0.7 0.0 copy-start.3
  0.7 0.0 copy-start.4
  0.7 0.1 copy.7.pairs
  0.8 0.6 copy-done.3
  1.4 0.0 copy-done.4
  1.4 0.0 copy-start
  1.4 1.0 copy-done
  2.4 0.0 copy-start.1
  2.4 1.0 copy-done.1
  3.5 0.0 copy-start.2
  3.5 0.9 copy-done.2
  4.4 123.1 %shard_map.64 = bf16[256,1024]{1,0:T(8,128)(2,1)S(1)} custom-call(bf16[256,1024]{1,0:T(8,128)(2,1)S(1)} %bitcast.5, bf16[256,1024]{1,0:T(8,128)(2,1)S(1)} %bitcast.6, bf16[8,128,128]{2,1,0:T(8,128)(2,1)S(1)} %bitcast.7, s32[16,4]{1,0:T(8,128)S(1)} %copy.7.pairs, f32[3,256]{1,0:T(4,128)S(1)} %copy-done.3, s32[3,256]{1,0:T(4,128)S(1)} %copy-done.4), custom_call_target="tpu_custom_call" | custom-call | flops 600000000 | bytes 2000000 | tf_op jit(solution)/shard_map/pallas_call | solution.py:456
  127.5 0.8 copy.9
Async XLA Ops:
  0.0 0.7 copy-start.5
  0.7 0.7 copy-start.3
  0.7 0.7 copy-start.4
  1.4 1.0 copy-start
  2.4 1.0 copy-start.1
  3.5 0.9 copy-start.2

commit v2 on v1

--- a/solution.py
+++ b/solution.py
@@ -56,11 +56,15 @@
     transmission,
     direction,
     out,
+    source_v,
+    prior_v,
     cur_a,
     cur_b,
-    emission,
     turned,
-    turned_s,
+    s_send,
+    s_recv,
+    ss_send,
+    ss_recv,
     blocks,
     coef_own,
     coef,
@@ -82,10 +86,13 @@
     c_send,
     f_send,
     f_recv,
+    in_sem,
     s0_send,
     s0_recv,
     gather_send,
     gather_recv,
+    direct_sem,
+    part_sem,
     x_sem,
     e_sem,
     b_sem,
@@ -111,8 +118,25 @@
     def await_bytes(ref, sem):
         pltpu.make_async_copy(ref, ref, sem).wait()
 
+    loads = [
+        pltpu.make_async_copy(prior, prior_v, in_sem.at[0]),
+        pltpu.make_async_copy(coupling, blocks.at[me_m], in_sem.at[1]),
+        pltpu.make_async_copy(source, source_v, in_sem.at[2]),
+    ]
+    for load in loads:
+        load.start()
+
     barrier = pltpu.get_barrier_semaphore()
     group = nm * ny_dev
+    far = nz_dev // 2
+
+    def greet_ring(j, carry):
+        step = far + jnp.where(j % 2 == 0, j // 2, -(j + 1) // 2)
+        z = (me_z + step) % nz_dev
+        pl.semaphore_signal(barrier, inc=1, device_id=(z * ny_dev + me_y, me_m), device_id_type=MESH)
+        return carry
+
+    lax.fori_loop(0, nz_dev - 1, greet_ring, 0)
 
     def greet_group(j, carry):
         m = (me_m + j // ny_dev) % nm
@@ -121,13 +145,6 @@
         return carry
 
     lax.fori_loop(1, group, greet_group, 0)
-
-    def greet_ring(j, carry):
-        z = (me_z + j) % nz_dev
-        pl.semaphore_signal(barrier, inc=1, device_id=(z * ny_dev + me_y, me_m), device_id_type=MESH)
-        return carry
-
-    lax.fori_loop(1, nz_dev, greet_ring, 0)
 
     fwd = {}
     fac = {}
@@ -147,22 +164,40 @@
 
     eye = identity(chunk)
 
-    def turn(array, into):
-        for m in range(nm):
-            for h in range(2):
-                tile = nt(eye, array[h * BLOCK : (h + 1) * BLOCK, m * chunk : (m + 1) * chunk])
-                rows = [
-                    tile[y * nz + zh * ZLO : y * nz + (zh + 1) * ZLO]
-                    for zh in range(ny_dev)
-                    for y in range(YLO)
-                ]
-                into[m, h] = jnp.concatenate(rows, axis=0).astype(BF16)
-
-    turn(prior, turned)
+    loads[0].wait()
+    for m in range(nm):
+        for h in range(2):
+            tile = nt(eye, prior_v[h * BLOCK : (h + 1) * BLOCK, m * chunk : (m + 1) * chunk])
+            rows = [
+                tile[y * nz + zh * ZLO : y * nz + (zh + 1) * ZLO] for zh in range(ny_dev) for y in range(YLO)
+            ]
+            turned[m, h] = jnp.concatenate(rows, axis=0).astype(BF16)
+
+    def sweep_z(factor, forward):
+        values = run([work[pl.ds(z, 8, stride=nz), :] for z in range(nz)], factor, forward)
+        largest = jnp.abs(values[0])
+        for z in range(nz):
+            work[pl.ds(z, 8, stride=nz), :] = values[z]
+            if z:
+                largest = jnp.maximum(largest, jnp.abs(values[z]))
+        largest = jnp.maximum(jnp.max(largest, axis=0, keepdims=True), 1e-30)
+        return TOP / largest, largest * (1.0 / TOP)
+
+    def two_rows(h, y, zh):
+        start = h * chunk + y * nz + zh * ZLO
+        return jnp.concatenate([work[start : start + ZLO, :], work[start + nz : start + nz + ZLO, :]], axis=0)
+
+    loads[1].wait()
     pl.semaphore_wait(barrier, group - 1 + nz_dev - 1)
 
-    local = pltpu.make_async_copy(turned.at[me_m], cur_a.at[me_m], s0_recv.at[0])
-    local.start()
+    sibling = me_x * 2 + 1 - me_core
+    shared = pl.ds(PER_ROW + me_y, 1)
+    direct = pl.ds(0, PER_ROW)
+    for j in range(1, chips):
+        to = (me_c, ((me_x + j) % chips) * 2 + me_core)
+        part = blocks.at[me_m, shared]
+        remote(part, part, gather_send.at[0], part_sem.at[j], to).start()
+    pltpu.make_async_copy(turned.at[me_m], cur_a.at[me_m], s0_recv.at[0]).start()
     for j in range(1, nm):
         m = (me_m + j) % nm
         remote(turned.at[m], cur_a.at[me_m], s0_send.at[0], s0_recv.at[0], (me_c, m)).start()
@@ -170,29 +205,59 @@
     for j in range(1, nm):
         m = (me_m + j) % nm
         remote(coef_own, coef.at[me_m], s0_send.at[2], s0_recv.at[2], (me_c, m)).start()
-    sibling = me_x * 2 + 1 - me_core
     for j in range(1, chips):
-        x = (me_x + j) % chips
-        remote(
-            coupling, blocks.at[me_m], gather_send.at[0], gather_recv.at[j], (me_c, x * 2 + me_core)
-        ).start()
-    remote(coupling, blocks.at[me_m], gather_send.at[1], gather_recv.at[0], (me_c, sibling)).start()
-    own_blocks = pltpu.make_async_copy(coupling, blocks.at[me_m], gather_send.at[3])
-    own_blocks.start()
-    turn(source, turned_s)
-    pltpu.make_async_copy(turned_s.at[me_m], emission.at[me_m], s0_recv.at[1]).start()
-    for j in range(1, nm):
-        m = (me_m + j) % nm
-        remote(turned_s.at[m], emission.at[me_m], s0_send.at[1], s0_recv.at[1], (me_c, m)).start()
+        to = (me_c, ((me_x + j) % chips) * 2 + me_core)
+        part = blocks.at[me_m, direct]
+        remote(part, part, gather_send.at[1], direct_sem.at[j], to).start()
+    own = blocks.at[me_m]
+    remote(own, own, gather_send.at[2], gather_recv.at[1], (me_c, sibling)).start()
+
+    def over_y(m):
+        part = blocks.at[m, shared]
+        for i in range(1, ny_dev):
+            to = (me_z * ny_dev + (me_y + i) % ny_dev, me_m)
+            remote(part, part, gather_send.at[3], gather_recv.at[0], to).start()
+
     for j in range(1, chips):
         m = ((me_x + chips - j) % chips) * 2 + me_core
-        await_bytes(blocks.at[m], gather_recv.at[j])
-        remote(blocks.at[m], blocks.at[m], gather_send.at[2], gather_recv.at[0], (me_c, sibling)).start()
-    own_blocks.wait()
+        await_bytes(blocks.at[m, shared], part_sem.at[j])
+        over_y(m)
+
+    loads[2].wait()
+
+    def sweep_source(m, carry):
+        for h in range(2):
+            columns = pl.ds(pl.multiple_of(m * chunk, chunk), chunk)
+            work[h * chunk : (h + 1) * chunk, :] = nt(eye, source_v[h * BLOCK : (h + 1) * BLOCK, columns])
+        scale, unit = sweep_z(coef_own[0], coef_own[1] > 0.5)
+        ss_send[m] = unit
+        for zh in range(ny_dev):
+            for h in range(2):
+                for y in range(0, YLO, 2):
+                    rows = pl.ds(m * YLO * ZLO + y * ZLO, 2 * ZLO)
+                    s_send[zh, h, rows, :] = encode(two_rows(h, y, zh), scale)
+        return carry
+
+    lax.fori_loop(0, nm, sweep_source, 0)
+    for i in range(1, ny_dev):
+        y = (me_y + i) % ny_dev
+        to = (me_z * ny_dev + y, me_m)
+        remote(s_send.at[y], s_recv.at[me_y], s0_send.at[1], s0_recv.at[1], to).start()
+        remote(ss_send, ss_recv.at[me_y], s0_send.at[3], s0_recv.at[3], to).start()
+    pltpu.make_async_copy(s_send.at[me_y], s_recv.at[me_y], s0_recv.at[1]).start()
+    pltpu.make_async_copy(ss_send, ss_recv.at[me_y], s0_recv.at[3]).start()
+    for j in range(1, chips):
+        part = blocks.at[((me_x + chips - j) % chips) * 2 + me_core, direct]
+        await_bytes(part, direct_sem.at[j])
+        remote(part, part, gather_send.at[4], gather_recv.at[1], (me_c, sibling)).start()
+    if chips > 1:
+        await_bytes(blocks.at[pl.ds(0, chips - 1), pl.ds(0, ny_dev - 1)], gather_recv.at[0])
+    for j in range(1, chips):
+        part = blocks.at[((me_x + chips - j) % chips) * 2 + me_core, pl.ds(PER_ROW, PER_ROW)]
+        remote(part, part, gather_send.at[4], gather_recv.at[1], (me_c, sibling)).start()
     await_bytes(cur_a, s0_recv.at[0])
     await_bytes(coef, s0_recv.at[2])
-    await_bytes(blocks.at[pl.ds(0, chips)], gather_recv.at[0])
-    await_bytes(emission, s0_recv.at[1])
+    await_bytes(blocks.at[pl.ds(0, chips)], gather_recv.at[1])
 
     for iteration in range(ITERS):
         current = cur_a if iteration == 0 else cur_b
@@ -204,32 +269,18 @@
                 row = m * 2 + h
                 left = jnp.concatenate([current[pairs[row, k] // 2, pairs[row, k] % 2] for k in range(PER_ROW)], axis=1)
                 right = jnp.concatenate([blocks[m, h * PER_ROW + k] for k in range(PER_ROW)], axis=1)
-                total = nt(left, right) + emission[m, h].astype(F32)
+                total = nt(left, right)
                 for zh in range(ny_dev):
                     for y in range(YLO):
                         work[h * chunk + y * nz + zh * ZLO : h * chunk + y * nz + (zh + 1) * ZLO, :] = total[
                             (zh * YLO + y) * ZLO : (zh * YLO + y + 1) * ZLO
                         ]
-            values = [work[pl.ds(z, 8, stride=nz), :] for z in range(nz)]
-            values = run(values, coef[m, 0], coef[m, 1] > 0.5)
-            largest = jnp.abs(values[0])
-            for z in range(nz):
-                work[pl.ds(z, 8, stride=nz), :] = values[z]
-                if z:
-                    largest = jnp.maximum(largest, jnp.abs(values[z]))
-            largest = jnp.maximum(jnp.max(largest, axis=0, keepdims=True), 1e-30)
-            xs_send[m] = largest * (1.0 / TOP)
-            scale = TOP / largest
+            scale, unit = sweep_z(coef[m, 0], coef[m, 1] > 0.5)
+            xs_send[m] = unit
             for zh in range(ny_dev):
                 for h in range(2):
                     for y in range(0, YLO, 2):
-                        rows = [
-                            work[h * chunk + (y + i) * nz + zh * ZLO : h * chunk + (y + i) * nz + (zh + 1) * ZLO, :]
-                            for i in range(2)
-                        ]
-                        x_send[m * ny_dev + zh, h, y * ZLO : (y + 2) * ZLO, :] = encode(
-                            jnp.concatenate(rows, axis=0), scale
-                        )
+                        x_send[m * ny_dev + zh, h, y * ZLO : (y + 2) * ZLO, :] = encode(two_rows(h, y, zh), scale)
             slot = me_m * ny_dev + me_y
             for i in range(ny_dev):
                 y = (me_y + 1 + i) % ny_dev
@@ -253,14 +304,18 @@
         lax.fori_loop(0, nm, scatter, 0)
         await_bytes(x_recv, x_sem.at[1])
         await_bytes(xs_recv, scale_sem.at[1])
+        if iteration == 0:
+            await_bytes(s_recv, s0_recv.at[1])
+            await_bytes(ss_recv, s0_recv.at[3])
 
         def unpack(m, carry):
             for h in range(2):
                 got = []
                 for x in range(XLO):
-                    factor = xs_recv[m * ny_dev + x] * weight[h]
-                    value = decode(x_recv[m * ny_dev + x, h]) * factor
-                    planes[h, x, pl.ds(m * YLO * ZLO, YLO * ZLO), :] = value
+                    rows = pl.ds(m * YLO * ZLO, YLO * ZLO)
+                    value = decode(x_recv[m * ny_dev + x, h]) * (xs_recv[m * ny_dev + x] * weight[h])
+                    value += decode(s_recv[x, h, rows, :]) * (ss_recv[x, m] * weight[h])
+                    planes[h, x, rows, :] = value
                     got.append(value)
                 t = jnp.concatenate([fac[0, h]] * YLO, axis=0)
                 f = jnp.concatenate([transmission_dir(h)] * YLO, axis=0) == 1
@@ -425,12 +480,15 @@
         remote(f_send.at[y], f_recv.at[me_y], f_sem.at[0], f_sem.at[1], (me_z * ny_dev + y, me_m)).start()
     pltpu.make_async_copy(f_send.at[me_y], f_recv.at[me_y], f_sem.at[1]).start()
     await_bytes(turned.at[pl.ds(0, nm - 1)], s0_send.at[0])
-    await_bytes(turned_s.at[pl.ds(0, nm - 1)], s0_send.at[1])
+    await_bytes(s_send.at[pl.ds(0, ny_dev - 1)], s0_send.at[1])
+    await_bytes(ss_recv.at[pl.ds(0, ny_dev - 1)], s0_send.at[3])
     await_bytes(coef.at[pl.ds(0, nm - 1)], s0_send.at[2])
     if chips > 1:
-        await_bytes(blocks.at[pl.ds(0, chips - 1)], gather_send.at[0])
-        await_bytes(blocks.at[pl.ds(0, chips - 1)], gather_send.at[2])
-    await_bytes(coupling, gather_send.at[1])
+        await_bytes(blocks.at[0, pl.ds(0, chips - 1)], gather_send.at[0])
+        await_bytes(blocks.at[pl.ds(0, chips - 1), direct], gather_send.at[1])
+        await_bytes(blocks.at[pl.ds(0, chips - 1), pl.ds(0, ny_dev - 1)], gather_send.at[3])
+        await_bytes(blocks.at[pl.ds(0, chips - 1)], gather_send.at[4])
+    await_bytes(blocks.at[0], gather_send.at[2])
     await_bytes(f_recv, f_sem.at[1])
     wide = identity(BLOCK)
     for m in range(nm):
@@ -452,18 +510,23 @@
     tall = ny * ZLO
     per_z = tall // nz_dev
     vmem = pl.BlockSpec(memory_space=pltpu.VMEM)
+    hbm = pl.BlockSpec(memory_space=pl.ANY)
     dma = pltpu.SemaphoreType.DMA
     result = pl.pallas_call(
         functools.partial(kernel, dims),
         out_shape=jax.ShapeDtypeStruct((modes, ny * nz), BF16),
-        in_specs=[vmem, vmem, vmem, pl.BlockSpec(memory_space=pltpu.SMEM), vmem, vmem],
+        in_specs=[hbm, hbm, hbm, pl.BlockSpec(memory_space=pltpu.SMEM), vmem, vmem],
         out_specs=vmem,
         scratch_shapes=[
+            pltpu.VMEM((modes, ny * nz), BF16),
+            pltpu.VMEM((modes, ny * nz), BF16),
             pltpu.VMEM((nm, 2, chunk, BLOCK), BF16),
             pltpu.VMEM((nm, 2, chunk, BLOCK), BF16),
             pltpu.VMEM((nm, 2, chunk, BLOCK), BF16),
-            pltpu.VMEM((nm, 2, chunk, BLOCK), BF16),
-            pltpu.VMEM((nm, 2, chunk, BLOCK), BF16),
+            pltpu.VMEM((ny_dev, 2, tall, BLOCK), I16),
+            pltpu.VMEM((ny_dev, 2, tall, BLOCK), I16),
+            pltpu.VMEM((nm, 1, BLOCK), F32),
+            pltpu.VMEM((ny_dev, nm, 1, BLOCK), F32),
             pltpu.VMEM((nm, 2 * PER_ROW, BLOCK, BLOCK), BF16),
             pltpu.VMEM((2, 8, BLOCK), F32),
             pltpu.VMEM((nm, 2, 8, BLOCK), F32),
@@ -486,8 +549,11 @@
             pltpu.VMEM((ny_dev, 2, tall, BLOCK), BF16),
             pltpu.VMEM((ny_dev, 2, tall, BLOCK), BF16),
             dma((3,)),
-            dma((3,)),
             dma((4,)),
+            dma((4,)),
+            dma((5,)),
+            dma((2,)),
+            dma((nm // 2,)),
             dma((nm // 2,)),
             dma((2,)),
             dma((2,)),

time: 129 us -> 125 us (0.969); the launches traced: 128 us -> 123 us
  Pallas kernels: 123 us -> 118 us
    pallas_call x1, Pallas kernels: 123 us -> 118 us  [local(): pl.pallas_call(functools.partial(kernel, dims), out_shape=jax.ShapeDtypeS...]
where the time goes in v2:
time: 125 us; the launch traced here: 123 us
  Pallas kernels  118 us (94%)
  local copies, waits for them, and re-layouts  5.21 us (4%)
    pallas_call x1, Pallas kernels, local(): pl.pallas_call(functools.partial(kernel, dims), out_shape=jax.ShapeDtypeS...  118 us
    unnamed x14, local copies, waits for them, and re-layouts  5.21 us

profile of v2, /device:TPU:6, one launch (start us, length us, event | category | flops | bytes accessed | tf_op | source)
XLA Modules:
  0.0 122.9 jit_solution(10173066849593813184)
XLA Ops:
  0.0 0.0 copy-start.5
  0.0 0.7 copy-done.5
  0.7 0.0 copy-start.3
  0.7 0.0 copy-start.4
  0.7 0.1 copy.7.pairs
  0.8 0.6 copy-done.3
  1.4 0.0 copy-done.4
  1.4 0.0 copy-start
  1.4 1.0 copy-done
  2.4 0.0 copy-start.1
  2.4 1.0 copy-done.1
  3.5 0.0 copy-start.2
  3.5 0.9 copy-done.2
  4.4 117.7 %shard_map.64 = bf16[256,1024]{1,0:T(8,128)(2,1)S(1)} custom-call(bf16[256,1024]{1,0:T(8,128)(2,1)S(1)} %bitcast.5, bf16[256,1024]{1,0:T(8,128)(2,1)S(1)} %bitcast.6, bf16[8,128,128]{2,1,0:T(8,128)(2,1)S(1)} %bitcast.7, s32[16,4]{1,0:T(8,128)S(1)} %copy.7.pairs, f32[3,256]{1,0:T(4,128)S(1)} %copy-done.3, s32[3,256]{1,0:T(4,128)S(1)} %copy-done.4), custom_call_target="tpu_custom_call" | custom-call | flops 600000000 | bytes 2000000 | tf_op jit(solution)/shard_map/pallas_call | solution.py:515
  122.1 0.8 copy.9
Async XLA Ops:
  0.0 0.7 copy-start.5
  0.7 0.7 copy-start.3
  0.7 0.7 copy-start.4
  1.4 1.0 copy-start
  2.4 1.0 copy-start.1
  3.5 0.9 copy-start.2

commit v3 on v2

--- a/solution.py
+++ b/solution.py
@@ -197,10 +197,10 @@
         to = (me_c, ((me_x + j) % chips) * 2 + me_core)
         part = blocks.at[me_m, shared]
         remote(part, part, gather_send.at[0], part_sem.at[j], to).start()
-    pltpu.make_async_copy(turned.at[me_m], cur_a.at[me_m], s0_recv.at[0]).start()
+    pltpu.make_async_copy(turned.at[me_m], cur_a.at[:, me_m], s0_recv.at[0]).start()
     for j in range(1, nm):
         m = (me_m + j) % nm
-        remote(turned.at[m], cur_a.at[me_m], s0_send.at[0], s0_recv.at[0], (me_c, m)).start()
+        remote(turned.at[m], cur_a.at[:, me_m], s0_send.at[0], s0_recv.at[0], (me_c, m)).start()
     pltpu.make_async_copy(coef_own, coef.at[me_m], s0_recv.at[2]).start()
     for j in range(1, nm):
         m = (me_m + j) % nm
@@ -267,7 +267,7 @@
             m = (me_m + 1 + j) % nm
             for h in range(2):
                 row = m * 2 + h
-                left = jnp.concatenate([current[pairs[row, k] // 2, pairs[row, k] % 2] for k in range(PER_ROW)], axis=1)
+                left = jnp.concatenate([current[pairs[row, k] % 2, pairs[row, k] // 2] for k in range(PER_ROW)], axis=1)
                 right = jnp.concatenate([blocks[m, h * PER_ROW + k] for k in range(PER_ROW)], axis=1)
                 total = nt(left, right)
                 for zh in range(ny_dev):
@@ -280,85 +280,97 @@
             for zh in range(ny_dev):
                 for h in range(2):
                     for y in range(0, YLO, 2):
-                        x_send[m * ny_dev + zh, h, y * ZLO : (y + 2) * ZLO, :] = encode(two_rows(h, y, zh), scale)
+                        x_send[h, m * ny_dev + zh, y * ZLO : (y + 2) * ZLO, :] = encode(two_rows(h, y, zh), scale)
+            send_codes(j, 0, True)
+            return carry
+
+        def send_codes(j, h, with_scale):
+            m = (me_m + 1 + j) % nm
             slot = me_m * ny_dev + me_y
             for i in range(ny_dev):
                 y = (me_y + 1 + i) % ny_dev
                 to = (me_z * ny_dev + y, m)
 
                 def send():
-                    remote(x_send.at[m * ny_dev + y], x_recv.at[slot], x_sem.at[0], x_sem.at[1], to).start()
-                    remote(xs_send.at[m], xs_recv.at[slot], scale_sem.at[0], scale_sem.at[1], to).start()
+                    src, dst = x_send.at[h, m * ny_dev + y], x_recv.at[h, slot]
+                    remote(src, dst, x_sem.at[h], x_sem.at[2 + h], to).start()
+                    if with_scale:
+                        remote(xs_send.at[m], xs_recv.at[slot], scale_sem.at[0], scale_sem.at[1], to).start()
 
                 def keep():
-                    pltpu.make_async_copy(x_send.at[m * ny_dev + y], x_recv.at[slot], x_sem.at[1]).start()
-                    pltpu.make_async_copy(xs_send.at[m], xs_recv.at[slot], scale_sem.at[1]).start()
+                    src, dst = x_send.at[h, m * ny_dev + y], x_recv.at[h, slot]
+                    pltpu.make_async_copy(src, dst, x_sem.at[2 + h]).start()
+                    if with_scale:
+                        pltpu.make_async_copy(xs_send.at[m], xs_recv.at[slot], scale_sem.at[1]).start()
 
                 if i < ny_dev - 1:
                     send()
                 else:
                     pl.when(j < nm - 1)(send)
                     pl.when(j == nm - 1)(keep)
+
+        def send_second(j, carry):
+            send_codes(j, 1, False)
             return carry
 
         lax.fori_loop(0, nm, scatter, 0)
-        await_bytes(x_recv, x_sem.at[1])
-        await_bytes(xs_recv, scale_sem.at[1])
-        if iteration == 0:
-            await_bytes(s_recv, s0_recv.at[1])
-            await_bytes(ss_recv, s0_recv.at[3])
-
-        def unpack(m, carry):
-            for h in range(2):
+        lax.fori_loop(0, nm, send_second, 0)
+
+        def send_ring(h, scale, codes, into, sem, unit, units, unit_sem):
+            def one(j, carry):
+                z = (me_z + 1 + j) % nz_dev
+                codes[h, z] = encode(ends[h, pl.ds(z * per_z, per_z), :], scale)
+                to = (z * ny_dev + me_y, me_m)
+
+                @pl.when(j < nz_dev - 1)
+                def _():
+                    remote(codes.at[h, z], into.at[h, me_z], sem.at[h], sem.at[2 + h], to).start()
+                    remote(
+                        unit.at[h], units.at[h, me_z], scale_sem.at[unit_sem + h], scale_sem.at[unit_sem + 2 + h], to
+                    ).start()
+
+                @pl.when(j == nz_dev - 1)
+                def _():
+                    pltpu.make_async_copy(codes.at[h, z], into.at[h, me_z], sem.at[2 + h]).start()
+                    pltpu.make_async_copy(unit.at[h], units.at[h, me_z], scale_sem.at[unit_sem + 2 + h]).start()
+
+                return carry
+
+            lax.fori_loop(0, nz_dev, one, 0)
+
+        def wide_fac(h):
+            return jnp.concatenate([fac[0, h]] * YLO, axis=0)
+
+        def wide_fwd(h):
+            tile = jnp.broadcast_to(direction[0:1, h * BLOCK : (h + 1) * BLOCK], (8, BLOCK))
+            return jnp.concatenate([tile] * YLO, axis=0) == 1
+
+        def hand_on(h):
+            def unpack(m, carry):
+                rows = pl.ds(m * YLO * ZLO, YLO * ZLO)
                 got = []
                 for x in range(XLO):
-                    rows = pl.ds(m * YLO * ZLO, YLO * ZLO)
-                    value = decode(x_recv[m * ny_dev + x, h]) * (xs_recv[m * ny_dev + x] * weight[h])
+                    value = decode(x_recv[h, m * ny_dev + x]) * (xs_recv[m * ny_dev + x] * weight[h])
                     value += decode(s_recv[x, h, rows, :]) * (ss_recv[x, m] * weight[h])
                     planes[h, x, rows, :] = value
                     got.append(value)
-                t = jnp.concatenate([fac[0, h]] * YLO, axis=0)
-                f = jnp.concatenate([transmission_dir(h)] * YLO, axis=0) == 1
+                t, f = wide_fac(h), wide_fwd(h)
                 end = jnp.where(f, got[0], got[XLO - 1])
                 for x in range(1, XLO):
                     end = end * t + jnp.where(f, got[x], got[XLO - 1 - x])
-                ends[h, pl.ds(m * YLO * ZLO, YLO * ZLO), :] = end
-            return carry
-
-        def transmission_dir(h):
-            return jnp.broadcast_to(direction[0:1, h * BLOCK : (h + 1) * BLOCK], (8, BLOCK))
-
-        lax.fori_loop(0, nm, unpack, 0)
-        largest = jnp.full((8, BLOCK), 1e-30, F32)
-        for h in range(2):
+                ends[h, rows, :] = end
+                return carry
+
+            lax.fori_loop(0, nm, unpack, 0)
             values = [ends[h, y * ZLO : (y + 1) * ZLO, :] for y in range(ny)]
             values = run(values, fac[1, h], fwd[1, h])
+            largest = jnp.full((8, BLOCK), 1e-30, F32)
             for y in range(ny):
                 ends[h, y * ZLO : (y + 1) * ZLO, :] = values[y]
                 largest = jnp.maximum(largest, jnp.abs(values[y]))
-        largest = jnp.max(largest, axis=0, keepdims=True)
-        es_send[...] = largest * (1.0 / TOP)
-        scale = TOP / largest
-
-        def send_ends(j, carry):
-            z = (me_z + 1 + j) % nz_dev
-            for h in range(2):
-                e_send[z, h] = encode(ends[h, pl.ds(z * per_z, per_z), :], scale)
-            to = (z * ny_dev + me_y, me_m)
-
-            @pl.when(j < nz_dev - 1)
-            def _():
-                remote(e_send.at[z], e_recv.at[me_z], e_sem.at[0], e_sem.at[1], to).start()
-                remote(es_send, es_recv.at[me_z], scale_sem.at[2], scale_sem.at[3], to).start()
-
-            @pl.when(j == nz_dev - 1)
-            def _():
-                pltpu.make_async_copy(e_send.at[z], e_recv.at[me_z], e_sem.at[1]).start()
-                pltpu.make_async_copy(es_send, es_recv.at[me_z], scale_sem.at[3]).start()
-
-            return carry
-
-        lax.fori_loop(0, nz_dev, send_ends, 0)
+            largest = jnp.max(largest, axis=0, keepdims=True)
+            es_send[h] = largest * (1.0 / TOP)
+            send_ring(h, TOP / largest, e_send, e_recv, e_sem, es_send, es_recv, 2)
 
         def sweep_y(h):
             def one(x, carry):
@@ -370,20 +382,16 @@
 
             lax.fori_loop(0, XLO, one, 0)
 
-        sweep_y(0)
-        await_bytes(e_recv, e_sem.at[1])
-        await_bytes(es_recv, scale_sem.at[3])
-
-        largest = jnp.full((8, BLOCK), 1e-30, F32)
-        for h in range(2):
+        def scan_ring(h):
+            largest = jnp.full((8, BLOCK), 1e-30, F32)
             leap = fac[0, h] * fac[0, h]
             leap = leap * leap
+            f = fwd[0, h]
             for part in range(per_z // 16):
                 got = [
-                    decode(e_recv[z, h, part * 16 : part * 16 + 16, :]) * es_recv[z] for z in range(nz_dev)
+                    decode(e_recv[h, z, part * 16 : part * 16 + 16, :]) * es_recv[h, z] for z in range(nz_dev)
                 ]
                 for i in range(2):
-                    f = fwd[0, h]
                     given = [g[i * 8 : i * 8 + 8] for g in got]
                     ordered = [jnp.where(f, given[s], given[nz_dev - 1 - s]) for s in range(nz_dev)]
                     taken = [jnp.zeros_like(ordered[0])]
@@ -391,48 +399,24 @@
                         taken.append(leap * taken[-1] + ordered[s])
                     for z in range(nz_dev):
                         value = jnp.where(f, taken[z], taken[nz_dev - 1 - z])
-                        ends[h, z * per_z + part * 16 + i * 8 : z * per_z + part * 16 + i * 8 + 8, :] = value
+                        start = z * per_z + part * 16 + i * 8
+                        ends[h, start : start + 8, :] = value
                         largest = jnp.maximum(largest, jnp.abs(value))
-        largest = jnp.max(largest, axis=0, keepdims=True)
-        bs_send[...] = largest * (1.0 / TOP)
-        scale = TOP / largest
-
-        def send_back(j, carry):
-            z = (me_z + 1 + j) % nz_dev
-            for h in range(2):
-                b_send[z, h] = encode(ends[h, pl.ds(z * per_z, per_z), :], scale)
-            to = (z * ny_dev + me_y, me_m)
-
-            @pl.when(j < nz_dev - 1)
-            def _():
-                remote(b_send.at[z], b_recv.at[me_z], b_sem.at[0], b_sem.at[1], to).start()
-                remote(bs_send, bs_recv.at[me_z], scale_sem.at[4], scale_sem.at[5], to).start()
-
-            @pl.when(j == nz_dev - 1)
-            def _():
-                pltpu.make_async_copy(b_send.at[z], b_recv.at[me_z], b_sem.at[1]).start()
-                pltpu.make_async_copy(bs_send, bs_recv.at[me_z], scale_sem.at[5]).start()
-
-            return carry
-
-        lax.fori_loop(0, nz_dev, send_back, 0)
-        sweep_y(1)
-        await_bytes(b_recv, b_sem.at[1])
-        await_bytes(bs_recv, scale_sem.at[5])
-
-        def inflow(z, carry):
-            for h in range(2):
-                ends[h, pl.ds(z * per_z, per_z), :] = decode(b_recv[z, h]) * bs_recv[z]
-            return carry
-
-        lax.fori_loop(0, nz_dev, inflow, 0)
-
-        def finish(j, carry):
-            m = (me_m + 1 + j) % nm
-            rows = pl.ds(m * YLO * ZLO, YLO * ZLO)
-            for h in range(2):
-                t = jnp.concatenate([fac[0, h]] * YLO, axis=0)
-                f = jnp.concatenate([transmission_dir(h)] * YLO, axis=0) == 1
+            largest = jnp.max(largest, axis=0, keepdims=True)
+            bs_send[h] = largest * (1.0 / TOP)
+            send_ring(h, TOP / largest, b_send, b_recv, b_sem, bs_send, bs_recv, 6)
+
+        def finish_half(h):
+            def inflow(z, carry):
+                ends[h, pl.ds(z * per_z, per_z), :] = decode(b_recv[h, z]) * bs_recv[h, z]
+                return carry
+
+            lax.fori_loop(0, nz_dev, inflow, 0)
+
+            def finish(j, carry):
+                m = (me_m + 1 + j) % nm
+                rows = pl.ds(m * YLO * ZLO, YLO * ZLO)
+                t, f = wide_fac(h), wide_fwd(h)
                 given = [planes[h, x, rows, :] for x in range(XLO)]
                 value = ends[h, rows, :]
                 swept = []
@@ -442,43 +426,67 @@
                 for x in range(XLO):
                     result = jnp.where(f, swept[x], swept[XLO - 1 - x]).astype(BF16)
                     if last:
-                        f_send[x, h, rows, :] = result
+                        f_send[h, x, rows, :] = result
                     else:
-                        c_send[m * ny_dev + x, h] = result
-            if not last:
-                for i in range(ny_dev):
-                    y = (me_y + 1 + i) % ny_dev
-                    to = (me_z * ny_dev + y, m)
-                    into = cur_b.at[me_m, :, pl.ds(me_y * YLO * ZLO, YLO * ZLO), :]
-
-                    def send():
-                        remote(c_send.at[m * ny_dev + y], into, c_sem.at[0], c_sem.at[1], to).start()
-
-                    def keep():
-                        pltpu.make_async_copy(c_send.at[m * ny_dev + y], into, c_sem.at[1]).start()
-
-                    if i < ny_dev - 1:
-                        send()
-                    else:
-                        pl.when(j < nm - 1)(send)
-                        pl.when(j == nm - 1)(keep)
-            return carry
-
-        lax.fori_loop(0, nm, finish, 0)
-        await_bytes(x_send.at[pl.ds(0, group - 1)], x_sem.at[0])
+                        c_send[h, m * ny_dev + x] = result
+                if not last:
+                    for i in range(ny_dev):
+                        y = (me_y + 1 + i) % ny_dev
+                        to = (me_z * ny_dev + y, m)
+                        into = cur_b.at[h, me_m, pl.ds(me_y * YLO * ZLO, YLO * ZLO), :]
+
+                        def send():
+                            remote(c_send.at[h, m * ny_dev + y], into, c_sem.at[h], c_sem.at[2 + h], to).start()
+
+                        def keep():
+                            pltpu.make_async_copy(c_send.at[h, m * ny_dev + y], into, c_sem.at[2 + h]).start()
+
+                        if i < ny_dev - 1:
+                            send()
+                        else:
+                            pl.when(j < nm - 1)(send)
+                            pl.when(j == nm - 1)(keep)
+                return carry
+
+            lax.fori_loop(0, nm, finish, 0)
+            if last:
+                for i in range(1, ny_dev):
+                    y = (me_y + i) % ny_dev
+                    to = (me_z * ny_dev + y, me_m)
+                    remote(f_send.at[h, y], f_recv.at[h, me_y], f_sem.at[h], f_sem.at[2 + h], to).start()
+                pltpu.make_async_copy(f_send.at[h, me_y], f_recv.at[h, me_y], f_sem.at[2 + h]).start()
+
+        await_bytes(x_recv.at[0], x_sem.at[2])
+        await_bytes(xs_recv, scale_sem.at[1])
+        if iteration == 0:
+            await_bytes(s_recv, s0_recv.at[1])
+            await_bytes(ss_recv, s0_recv.at[3])
+        hand_on(0)
+        await_bytes(x_recv.at[1], x_sem.at[3])
+        hand_on(1)
+        sweep_y(0)
+        for h in range(2):
+            await_bytes(e_recv.at[h], e_sem.at[2 + h])
+            await_bytes(es_recv.at[h], scale_sem.at[4 + h])
+            scan_ring(h)
+            if h == 0:
+                sweep_y(1)
+        for h in range(2):
+            await_bytes(b_recv.at[h], b_sem.at[2 + h])
+            await_bytes(bs_recv.at[h], scale_sem.at[8 + h])
+            finish_half(h)
         await_bytes(xs_recv.at[pl.ds(0, group - 1)], scale_sem.at[0])
-        await_bytes(e_send.at[pl.ds(0, nz_dev - 1)], e_sem.at[0])
-        await_bytes(es_recv.at[pl.ds(0, nz_dev - 1)], scale_sem.at[2])
-        await_bytes(b_send.at[pl.ds(0, nz_dev - 1)], b_sem.at[0])
-        await_bytes(bs_recv.at[pl.ds(0, nz_dev - 1)], scale_sem.at[4])
+        for h in range(2):
+            await_bytes(x_send.at[h, pl.ds(0, group - 1)], x_sem.at[h])
+            await_bytes(e_send.at[h, pl.ds(0, nz_dev - 1)], e_sem.at[h])
+            await_bytes(es_recv.at[h, pl.ds(0, nz_dev - 1)], scale_sem.at[2 + h])
+            await_bytes(b_send.at[h, pl.ds(0, nz_dev - 1)], b_sem.at[h])
+            await_bytes(bs_recv.at[h, pl.ds(0, nz_dev - 1)], scale_sem.at[6 + h])
         if not last:
-            await_bytes(cur_b, c_sem.at[1])
-            await_bytes(c_send.at[pl.ds(0, group - 1)], c_sem.at[0])
-
-    for i in range(1, ny_dev):
-        y = (me_y + i) % ny_dev
-        remote(f_send.at[y], f_recv.at[me_y], f_sem.at[0], f_sem.at[1], (me_z * ny_dev + y, me_m)).start()
-    pltpu.make_async_copy(f_send.at[me_y], f_recv.at[me_y], f_sem.at[1]).start()
+            for h in range(2):
+                await_bytes(cur_b.at[h], c_sem.at[2 + h])
+                await_bytes(c_send.at[h, pl.ds(0, group - 1)], c_sem.at[h])
+
     await_bytes(turned.at[pl.ds(0, nm - 1)], s0_send.at[0])
     await_bytes(s_send.at[pl.ds(0, ny_dev - 1)], s0_send.at[1])
     await_bytes(ss_recv.at[pl.ds(0, ny_dev - 1)], s0_send.at[3])
@@ -489,17 +497,16 @@
         await_bytes(blocks.at[pl.ds(0, chips - 1), pl.ds(0, ny_dev - 1)], gather_send.at[3])
         await_bytes(blocks.at[pl.ds(0, chips - 1)], gather_send.at[4])
     await_bytes(blocks.at[0], gather_send.at[2])
-    await_bytes(f_recv, f_sem.at[1])
     wide = identity(BLOCK)
-    for m in range(nm):
-        for h in range(2):
-            parts = []
-            for zh in range(ny_dev):
-                parts.append(f_recv[zh, h, m * YLO * ZLO : (m + 1) * YLO * ZLO, :].astype(F32))
+    for h in range(2):
+        await_bytes(f_recv.at[h], f_sem.at[2 + h])
+        for m in range(nm):
+            parts = [f_recv[h, zh, m * YLO * ZLO : (m + 1) * YLO * ZLO, :].astype(F32) for zh in range(ny_dev)]
             rows = [parts[zh][y * ZLO : (y + 1) * ZLO] for y in range(YLO) for zh in range(ny_dev)]
             tile = jnp.concatenate(rows, axis=0).astype(BF16)
             out[h * BLOCK : (h + 1) * BLOCK, m * chunk : (m + 1) * chunk] = nt(wide, tile).astype(BF16)
-    await_bytes(f_send.at[pl.ds(0, ny_dev - 1)], f_sem.at[0])
+    for h in range(2):
+        await_bytes(f_send.at[h, pl.ds(0, ny_dev - 1)], f_sem.at[h])
 
 
 def local(dims, source, prior, coupling, pairs, transmission, direction):
@@ -510,7 +517,7 @@
     tall = ny * ZLO
     per_z = tall // nz_dev
     vmem = pl.BlockSpec(memory_space=pltpu.VMEM)
-    hbm = pl.BlockSpec(memory_space=pl.ANY)
+    hbm = pl.BlockSpec(memory_space=pltpu.HBM)
     dma = pltpu.SemaphoreType.DMA
     result = pl.pallas_call(
         functools.partial(kernel, dims),
@@ -520,8 +527,8 @@
         scratch_shapes=[
             pltpu.VMEM((modes, ny * nz), BF16),
             pltpu.VMEM((modes, ny * nz), BF16),
-            pltpu.VMEM((nm, 2, chunk, BLOCK), BF16),
-            pltpu.VMEM((nm, 2, chunk, BLOCK), BF16),
+            pltpu.VMEM((2, nm, chunk, BLOCK), BF16),
+            pltpu.VMEM((2, nm, chunk, BLOCK), BF16),
             pltpu.VMEM((nm, 2, chunk, BLOCK), BF16),
             pltpu.VMEM((ny_dev, 2, tall, BLOCK), I16),
             pltpu.VMEM((ny_dev, 2, tall, BLOCK), I16),
@@ -531,23 +538,23 @@
             pltpu.VMEM((2, 8, BLOCK), F32),
             pltpu.VMEM((nm, 2, 8, BLOCK), F32),
             pltpu.VMEM((2 * chunk, BLOCK), F32),
-            pltpu.VMEM((group, 2, YLO * ZLO, BLOCK), I16),
-            pltpu.VMEM((group, 2, YLO * ZLO, BLOCK), I16),
+            pltpu.VMEM((2, group, YLO * ZLO, BLOCK), I16),
+            pltpu.VMEM((2, group, YLO * ZLO, BLOCK), I16),
             pltpu.VMEM((nm, 1, BLOCK), F32),
             pltpu.VMEM((group, 1, BLOCK), F32),
             pltpu.VMEM((2, XLO, tall, BLOCK), F32),
             pltpu.VMEM((2, tall, BLOCK), F32),
-            pltpu.VMEM((nz_dev, 2, per_z, BLOCK), I16),
-            pltpu.VMEM((nz_dev, 2, per_z, BLOCK), I16),
-            pltpu.VMEM((1, BLOCK), F32),
-            pltpu.VMEM((nz_dev, 1, BLOCK), F32),
-            pltpu.VMEM((nz_dev, 2, per_z, BLOCK), I16),
-            pltpu.VMEM((nz_dev, 2, per_z, BLOCK), I16),
-            pltpu.VMEM((1, BLOCK), F32),
-            pltpu.VMEM((nz_dev, 1, BLOCK), F32),
-            pltpu.VMEM((group, 2, YLO * ZLO, BLOCK), BF16),
-            pltpu.VMEM((ny_dev, 2, tall, BLOCK), BF16),
-            pltpu.VMEM((ny_dev, 2, tall, BLOCK), BF16),
+            pltpu.VMEM((2, nz_dev, per_z, BLOCK), I16),
+            pltpu.VMEM((2, nz_dev, per_z, BLOCK), I16),
+            pltpu.VMEM((2, 1, BLOCK), F32),
+            pltpu.VMEM((2, nz_dev, 1, BLOCK), F32),
+            pltpu.VMEM((2, nz_dev, per_z, BLOCK), I16),
+            pltpu.VMEM((2, nz_dev, per_z, BLOCK), I16),
+            pltpu.VMEM((2, 1, BLOCK), F32),
+            pltpu.VMEM((2, nz_dev, 1, BLOCK), F32),
+            pltpu.VMEM((2, group, YLO * ZLO, BLOCK), BF16),
+            pltpu.VMEM((2, ny_dev, tall, BLOCK), BF16),
+            pltpu.VMEM((2, ny_dev, tall, BLOCK), BF16),
             dma((3,)),
             dma((4,)),
             dma((4,)),
@@ -555,12 +562,12 @@
             dma((2,)),
             dma((nm // 2,)),
             dma((nm // 2,)),
-            dma((2,)),
-            dma((2,)),
-            dma((2,)),
-            dma((2,)),
-            dma((2,)),
-            dma((6,)),
+            dma((4,)),
+            dma((4,)),
+            dma((4,)),
+            dma((4,)),
+            dma((4,)),
+            dma((10,)),
         ],
         compiler_params=pltpu.CompilerParams(
             collective_id=0, has_side_effects=True, vmem_limit_bytes=40 * 1024 * 1024

time: 125 us -> 113 us (0.904)
  Pallas kernels: 118 us -> 106 us
    pallas_call x1, Pallas kernels: 118 us -> 106 us  [local(): pl.pallas_call(functools.partial(kernel, dims), out_shape=jax.ShapeDtypeS...]
where the time goes in v3:
time: 113 us; the launch traced here: 111 us
  Pallas kernels  106 us (94%)
  local copies, waits for them, and re-layouts  5.21 us (5%)
    pallas_call x1, Pallas kernels, local(): pl.pallas_call(functools.partial(kernel, dims), out_shape=jax.ShapeDtypeS...  106 us
    unnamed x14, local copies, waits for them, and re-layouts  5.21 us

profile of v3, /device:TPU:6, one launch (start us, length us, event | category | flops | bytes accessed | tf_op | source)
XLA Modules:
  0.0 111.5 jit_solution(5397706182173629128)
XLA Ops:
  0.0 0.0 copy-start.5
  0.0 0.7 copy-done.5
  0.7 0.0 copy-start.3
  0.7 0.0 copy-start.4
  0.7 0.1 copy.7.pairs
  0.8 0.6 copy-done.3
  1.4 0.0 copy-done.4
  1.4 0.0 copy-start
  1.4 1.0 copy-done
  2.4 0.0 copy-start.1
  2.4 1.0 copy-done.1
  3.5 0.0 copy-start.2
  3.5 0.9 copy-done.2
  4.4 106.2 %shard_map.64 = bf16[256,1024]{1,0:T(8,128)(2,1)S(1)} custom-call(bf16[256,1024]{1,0:T(8,128)(2,1)S(1)} %bitcast.5, bf16[256,1024]{1,0:T(8,128)(2,1)S(1)} %bitcast.6, bf16[8,128,128]{2,1,0:T(8,128)(2,1)S(1)} %bitcast.7, s32[16,4]{1,0:T(8,128)S(1)} %copy.7.pairs, f32[3,256]{1,0:T(4,128)S(1)} %copy-done.3, s32[3,256]{1,0:T(4,128)S(1)} %copy-done.4), custom_call_target="tpu_custom_call" | custom-call | flops 600000000 | bytes 2000000 | tf_op jit(solution)/shard_map/pallas_call | solution.py:522
  110.7 0.8 copy.9
Async XLA Ops:
  0.0 0.7 copy-start.5
  0.7 0.7 copy-start.3
  0.7 0.7 copy-start.4
  1.4 1.0 copy-start
  2.4 1.0 copy-start.1
  3.5 0.9 copy-start.2

commit v4 on v3

--- a/solution.py
+++ b/solution.py
@@ -52,10 +52,13 @@
     source,
     prior,
     coupling,
+    pairs_in,
+    transmission_in,
+    direction_in,
+    out,
     pairs,
     transmission,
     direction,
-    out,
     source_v,
     prior_v,
     cur_a,
@@ -86,6 +89,7 @@
     c_send,
     f_send,
     f_recv,
+    round_sem,
     in_sem,
     s0_send,
     s0_recv,
@@ -123,29 +127,39 @@
         pltpu.make_async_copy(coupling, blocks.at[me_m], in_sem.at[1]),
         pltpu.make_async_copy(source, source_v, in_sem.at[2]),
     ]
-    for load in loads:
-        load.start()
+    small = [
+        pltpu.make_async_copy(transmission_in, transmission, in_sem.at[3]),
+        pltpu.make_async_copy(direction_in, direction, in_sem.at[4]),
+        pltpu.make_async_copy(pairs_in, pairs, in_sem.at[5]),
+    ]
 
     barrier = pltpu.get_barrier_semaphore()
     group = nm * ny_dev
-    far = nz_dev // 2
-
-    def greet_ring(j, carry):
-        step = far + jnp.where(j % 2 == 0, j // 2, -(j + 1) // 2)
-        z = (me_z + step) % nz_dev
-        pl.semaphore_signal(barrier, inc=1, device_id=(z * ny_dev + me_y, me_m), device_id_type=MESH)
-        return carry
-
-    lax.fori_loop(0, nz_dev - 1, greet_ring, 0)
-
-    def greet_group(j, carry):
-        m = (me_m + j // ny_dev) % nm
-        y = (me_y + j % ny_dev) % ny_dev
-        pl.semaphore_signal(barrier, inc=1, device_id=(me_z * ny_dev + y, m), device_id_type=MESH)
-        return carry
-
-    lax.fori_loop(1, group, greet_group, 0)
-
+    near = [(me_z * ny_dev + (me_y + i) % ny_dev, me_m) for i in range(1, ny_dev)]
+    near += [(me_c, (me_m + j) % nm) for j in range(1, nm)]
+
+    def ring(step):
+        return [((me_z + z) % nz_dev * ny_dev + me_y, me_m) for z in sorted({step % nz_dev, -step % nz_dev} - {0})]
+
+    near += ring(1)
+    for to in near:
+        pl.semaphore_signal(barrier, inc=1, device_id=to, device_id_type=MESH)
+    for load in small + loads:
+        load.start()
+
+    rounds = []
+    while 2 ** len(rounds) < nz_dev // 2:
+        rounds.append(2 ** len(rounds))
+
+    def meet(r):
+        if r and r - 1 < len(rounds):
+            pl.semaphore_wait(round_sem.at[r - 1], 2)
+        if r < len(rounds):
+            for to in ring(rounds[r]):
+                pl.semaphore_signal(round_sem.at[r], inc=1, device_id=to, device_id_type=MESH)
+
+    for load in small:
+        load.wait()
     fwd = {}
     fac = {}
     weight = {}
@@ -188,7 +202,8 @@
         return jnp.concatenate([work[start : start + ZLO, :], work[start + nz : start + nz + ZLO, :]], axis=0)
 
     loads[1].wait()
-    pl.semaphore_wait(barrier, group - 1 + nz_dev - 1)
+    pl.semaphore_wait(barrier, len(near))
+    meet(0)
 
     sibling = me_x * 2 + 1 - me_core
     shared = pl.ds(PER_ROW + me_y, 1)
@@ -218,11 +233,13 @@
             to = (me_z * ny_dev + (me_y + i) % ny_dev, me_m)
             remote(part, part, gather_send.at[3], gather_recv.at[0], to).start()
 
+    meet(1)
     for j in range(1, chips):
         m = ((me_x + chips - j) % chips) * 2 + me_core
         await_bytes(blocks.at[m, shared], part_sem.at[j])
         over_y(m)
 
+    meet(2)
     loads[2].wait()
 
     def sweep_source(m, carry):
@@ -255,6 +272,7 @@
     for j in range(1, chips):
         part = blocks.at[((me_x + chips - j) % chips) * 2 + me_core, pl.ds(PER_ROW, PER_ROW)]
         remote(part, part, gather_send.at[4], gather_recv.at[1], (me_c, sibling)).start()
+    meet(3)
     await_bytes(cur_a, s0_recv.at[0])
     await_bytes(coef, s0_recv.at[2])
     await_bytes(blocks.at[pl.ds(0, chips)], gather_recv.at[1])
@@ -267,7 +285,7 @@
             m = (me_m + 1 + j) % nm
             for h in range(2):
                 row = m * 2 + h
-                left = jnp.concatenate([current[pairs[row, k] % 2, pairs[row, k] // 2] for k in range(PER_ROW)], axis=1)
+                left = jnp.concatenate([current[pairs[k, row] % 2, pairs[k, row] // 2] for k in range(PER_ROW)], axis=1)
                 right = jnp.concatenate([blocks[m, h * PER_ROW + k] for k in range(PER_ROW)], axis=1)
                 total = nt(left, right)
                 for zh in range(ny_dev):
@@ -522,9 +540,12 @@
     result = pl.pallas_call(
         functools.partial(kernel, dims),
         out_shape=jax.ShapeDtypeStruct((modes, ny * nz), BF16),
-        in_specs=[hbm, hbm, hbm, pl.BlockSpec(memory_space=pltpu.SMEM), vmem, vmem],
+        in_specs=[hbm] * 6,
         out_specs=vmem,
         scratch_shapes=[
+            pltpu.SMEM((PER_ROW, 2 * nm), jnp.int32),
+            pltpu.VMEM((3, modes), F32),
+            pltpu.VMEM((3, modes), jnp.int32),
             pltpu.VMEM((modes, ny * nz), BF16),
             pltpu.VMEM((modes, ny * nz), BF16),
             pltpu.VMEM((2, nm, chunk, BLOCK), BF16),
@@ -555,7 +576,8 @@
             pltpu.VMEM((2, group, YLO * ZLO, BLOCK), BF16),
             pltpu.VMEM((2, ny_dev, tall, BLOCK), BF16),
             pltpu.VMEM((2, ny_dev, tall, BLOCK), BF16),
-            dma((3,)),
+            pltpu.SemaphoreType.REGULAR((4,)),
+            dma((6,)),
             dma((4,)),
             dma((4,)),
             dma((5,)),
@@ -570,14 +592,14 @@
             dma((10,)),
         ],
         compiler_params=pltpu.CompilerParams(
-            collective_id=0, has_side_effects=True, vmem_limit_bytes=40 * 1024 * 1024
+            collective_id=0, has_side_effects=True, vmem_limit_bytes=60 * 1024 * 1024
         ),
         cost_estimate=pl.CostEstimate(flops=600_000_000, bytes_accessed=2_000_000, transcendentals=0),
     )(
         source.reshape(modes, ny * nz),
         prior.reshape(modes, ny * nz),
         coupling.reshape(2 * PER_ROW, BLOCK, BLOCK),
-        pairs,
+        pairs.T,
         transmission,
         direction,
     )

time: 113 us -> 105 us (0.929); the launches traced: 111 us -> 105 us
  local copies, waits for them, and re-layouts: 5.21 us -> 1.87 us
  Pallas kernels: 106 us -> 103 us
    pallas_call x1, Pallas kernels: 106 us -> 103 us  [local(): pl.pallas_call(functools.partial(kernel, dims), out_shape=jax.ShapeDtypeS...]
    unnamed x14 -> x1, local copies, waits for them, and re-layouts: 5.21 us -> 1.87 us
where the time goes in v4:
time: 105 us
  Pallas kernels  103 us (98%)
  local copies, waits for them, and re-layouts  1.87 us (2%)
    pallas_call x1, Pallas kernels, local(): pl.pallas_call(functools.partial(kernel, dims), out_shape=jax.ShapeDtypeS...  103 us

profile of v4, /device:TPU:6, one launch (start us, length us, event | category | flops | bytes accessed | tf_op | source)
XLA Modules:
  0.0 104.6 jit_solution(14657740688239062181)
XLA Ops:
  0.0 102.7 %shard_map.64 = bf16[256,1024]{1,0:T(8,128)(2,1)} custom-call(bf16[256,1024]{1,0:T(8,128)(2,1)} %bitcast.6, bf16[256,1024]{1,0:T(8,128)(2,1)} %bitcast.7, bf16[8,128,128]{2,1,0:T(8,128)(2,1)} %bitcast.8, s32[4,16]{1,0:T(4,128)} %bitcast.9, f32[3,256]{1,0:T(4,128)} %transmission_in.1, s32[3,256]{1,0:T(4,128)} %direction_in.1), custom_call_target="tpu_custom_call" | custom-call | flops 600000000 | bytes 2000000 | tf_op jit(solution)/shard_map/pallas_call | solution.py:540
  102.7 1.9 %copy.8 = bf16[256,1,1024]{2,0,1:T(8,128)(2,1)} copy(bf16[256,1,1024]{2,0,1:T(8,128)(2,1)} %bitcast.5) | data formatting | bytes 1048576

commit v5 on v4

--- a/solution.py
+++ b/solution.py
@@ -37,6 +37,12 @@
     for s in range(1, n):
         swept.append(factor * swept[-1] + ordered[s])
     return [jnp.where(forward, swept[s], swept[n - 1 - s]) for s in range(n)]
+
+
+def farthest_first(j, n):
+    if isinstance(j, int):
+        return (n // 2 + (j // 2 if j % 2 == 0 else -((j + 1) // 2))) % n
+    return n // 2 + jnp.where(j % 2 == 0, j // 2, -((j + 1) // 2)) + n
 
 
 def encode(values, scale):
@@ -119,6 +125,13 @@
             src_ref=src, dst_ref=dst, send_sem=send, recv_sem=recv, device_id=to, device_id_type=MESH
         )
 
+    def mode_at(j):
+        x = (me_x + farthest_first(j // 2, chips)) % chips
+        return x * 2 + (me_core + 1 + j % 2) % 2
+
+    def y_at(i):
+        return (me_y + farthest_first(i, ny_dev)) % ny_dev
+
     def await_bytes(ref, sem):
         pltpu.make_async_copy(ref, ref, sem).wait()
 
@@ -208,19 +221,19 @@
     sibling = me_x * 2 + 1 - me_core
     shared = pl.ds(PER_ROW + me_y, 1)
     direct = pl.ds(0, PER_ROW)
-    for j in range(1, chips):
+    for j in [farthest_first(i, chips) for i in range(chips - 1)]:
         to = (me_c, ((me_x + j) % chips) * 2 + me_core)
         part = blocks.at[me_m, shared]
         remote(part, part, gather_send.at[0], part_sem.at[j], to).start()
     pltpu.make_async_copy(turned.at[me_m], cur_a.at[:, me_m], s0_recv.at[0]).start()
-    for j in range(1, nm):
-        m = (me_m + j) % nm
+    for j in range(nm - 1):
+        m = mode_at(j)
         remote(turned.at[m], cur_a.at[:, me_m], s0_send.at[0], s0_recv.at[0], (me_c, m)).start()
     pltpu.make_async_copy(coef_own, coef.at[me_m], s0_recv.at[2]).start()
-    for j in range(1, nm):
-        m = (me_m + j) % nm
+    for j in range(nm - 1):
+        m = mode_at(j)
         remote(coef_own, coef.at[me_m], s0_send.at[2], s0_recv.at[2], (me_c, m)).start()
-    for j in range(1, chips):
+    for j in [farthest_first(i, chips) for i in range(chips - 1)]:
         to = (me_c, ((me_x + j) % chips) * 2 + me_core)
         part = blocks.at[me_m, direct]
         remote(part, part, gather_send.at[1], direct_sem.at[j], to).start()
@@ -229,12 +242,12 @@
 
     def over_y(m):
         part = blocks.at[m, shared]
-        for i in range(1, ny_dev):
-            to = (me_z * ny_dev + (me_y + i) % ny_dev, me_m)
+        for i in range(ny_dev - 1):
+            to = (me_z * ny_dev + y_at(i), me_m)
             remote(part, part, gather_send.at[3], gather_recv.at[0], to).start()
 
     meet(1)
-    for j in range(1, chips):
+    for j in [farthest_first(i, chips) for i in range(chips - 1)]:
         m = ((me_x + chips - j) % chips) * 2 + me_core
         await_bytes(blocks.at[m, shared], part_sem.at[j])
         over_y(m)
@@ -256,8 +269,8 @@
         return carry
 
     lax.fori_loop(0, nm, sweep_source, 0)
-    for i in range(1, ny_dev):
-        y = (me_y + i) % ny_dev
+    for i in range(ny_dev - 1):
+        y = y_at(i)
         to = (me_z * ny_dev + y, me_m)
         remote(s_send.at[y], s_recv.at[me_y], s0_send.at[1], s0_recv.at[1], to).start()
         remote(ss_send, ss_recv.at[me_y], s0_send.at[3], s0_recv.at[3], to).start()
@@ -282,7 +295,7 @@
         last = iteration == ITERS - 1
 
         def scatter(j, carry):
-            m = (me_m + 1 + j) % nm
+            m = mode_at(j)
             for h in range(2):
                 row = m * 2 + h
                 left = jnp.concatenate([current[pairs[k, row] % 2, pairs[k, row] // 2] for k in range(PER_ROW)], axis=1)
@@ -303,10 +316,10 @@
             return carry
 
         def send_codes(j, h, with_scale):
-            m = (me_m + 1 + j) % nm
+            m = mode_at(j)
             slot = me_m * ny_dev + me_y
             for i in range(ny_dev):
-                y = (me_y + 1 + i) % ny_dev
+                y = y_at(i)
                 to = (me_z * ny_dev + y, m)
 
                 def send():
@@ -336,7 +349,7 @@
 
         def send_ring(h, scale, codes, into, sem, unit, units, unit_sem):
             def one(j, carry):
-                z = (me_z + 1 + j) % nz_dev
+                z = (me_z + farthest_first(j, nz_dev)) % nz_dev
                 codes[h, z] = encode(ends[h, pl.ds(z * per_z, per_z), :], scale)
                 to = (z * ny_dev + me_y, me_m)
 
@@ -432,7 +445,7 @@
             lax.fori_loop(0, nz_dev, inflow, 0)
 
             def finish(j, carry):
-                m = (me_m + 1 + j) % nm
+                m = mode_at(j)
                 rows = pl.ds(m * YLO * ZLO, YLO * ZLO)
                 t, f = wide_fac(h), wide_fwd(h)
                 given = [planes[h, x, rows, :] for x in range(XLO)]
@@ -449,7 +462,7 @@
                         c_send[h, m * ny_dev + x] = result
                 if not last:
                     for i in range(ny_dev):
-                        y = (me_y + 1 + i) % ny_dev
+                        y = y_at(i)
                         to = (me_z * ny_dev + y, m)
                         into = cur_b.at[h, me_m, pl.ds(me_y * YLO * ZLO, YLO * ZLO), :]
 
@@ -468,8 +481,8 @@
 
             lax.fori_loop(0, nm, finish, 0)
             if last:
-                for i in range(1, ny_dev):
-                    y = (me_y + i) % ny_dev
+                for i in range(ny_dev - 1):
+                    y = y_at(i)
                     to = (me_z * ny_dev + y, me_m)
                     remote(f_send.at[h, y], f_recv.at[h, me_y], f_sem.at[h], f_sem.at[2 + h], to).start()
                 pltpu.make_async_copy(f_send.at[h, me_y], f_recv.at[h, me_y], f_sem.at[2 + h]).start()

time: 105 us -> 98.3 us (0.936)
  Pallas kernels: 103 us -> 95.5 us
    pallas_call x1, Pallas kernels: 103 us -> 95.5 us  [local(): pl.pallas_call(functools.partial(kernel, dims), out_shape=jax.ShapeDtypeS...]
where the time goes in v5:
time: 98.3 us; the launch traced here: 97.4 us
  Pallas kernels  95.5 us (97%)
  local copies, waits for them, and re-layouts  1.87 us (2%)
    pallas_call x1, Pallas kernels, local(): pl.pallas_call(functools.partial(kernel, dims), out_shape=jax.ShapeDtypeS...  95.5 us

profile of v5, /device:TPU:6, one launch (start us, length us, event | category | flops | bytes accessed | tf_op | source)
XLA Modules:
  0.0 97.4 jit_solution(5929012969934133370)
XLA Ops:
  0.0 95.5 %shard_map.64 = bf16[256,1024]{1,0:T(8,128)(2,1)} custom-call(bf16[256,1024]{1,0:T(8,128)(2,1)} %bitcast.6, bf16[256,1024]{1,0:T(8,128)(2,1)} %bitcast.7, bf16[8,128,128]{2,1,0:T(8,128)(2,1)} %bitcast.8, s32[4,16]{1,0:T(4,128)} %bitcast.9, f32[3,256]{1,0:T(4,128)} %transmission_in.1, s32[3,256]{1,0:T(4,128)} %direction_in.1), custom_call_target="tpu_custom_call" | custom-call | flops 600000000 | bytes 2000000 | tf_op jit(solution)/shard_map/pallas_call | solution.py:553
  95.5 1.9 %copy.8 = bf16[256,1,1024]{2,0,1:T(8,128)(2,1)} copy(bf16[256,1,1024]{2,0,1:T(8,128)(2,1)} %bitcast.5) | data formatting | bytes 1048576

commit v6 on v5

--- a/solution.py
+++ b/solution.py
@@ -90,8 +90,7 @@
     es_recv,
     b_send,
     b_recv,
-    bs_send,
-    bs_recv,
+    bound,
     c_send,
     f_send,
     f_recv,
@@ -225,6 +224,10 @@
         to = (me_c, ((me_x + j) % chips) * 2 + me_core)
         part = blocks.at[me_m, shared]
         remote(part, part, gather_send.at[0], part_sem.at[j], to).start()
+    for j in [farthest_first(i, chips) for i in range(chips - 1)]:
+        to = (me_c, ((me_x + j) % chips) * 2 + me_core)
+        part = blocks.at[me_m, direct]
+        remote(part, part, gather_send.at[1], direct_sem.at[j], to).start()
     pltpu.make_async_copy(turned.at[me_m], cur_a.at[:, me_m], s0_recv.at[0]).start()
     for j in range(nm - 1):
         m = mode_at(j)
@@ -233,10 +236,6 @@
     for j in range(nm - 1):
         m = mode_at(j)
         remote(coef_own, coef.at[me_m], s0_send.at[2], s0_recv.at[2], (me_c, m)).start()
-    for j in [farthest_first(i, chips) for i in range(chips - 1)]:
-        to = (me_c, ((me_x + j) % chips) * 2 + me_core)
-        part = blocks.at[me_m, direct]
-        remote(part, part, gather_send.at[1], direct_sem.at[j], to).start()
     own = blocks.at[me_m]
     remote(own, own, gather_send.at[2], gather_recv.at[1], (me_c, sibling)).start()
 
@@ -347,23 +346,25 @@
         lax.fori_loop(0, nm, scatter, 0)
         lax.fori_loop(0, nm, send_second, 0)
 
-        def send_ring(h, scale, codes, into, sem, unit, units, unit_sem):
+        def send_ring(h, scale_of, codes, into, sem, with_unit):
             def one(j, carry):
                 z = (me_z + farthest_first(j, nz_dev)) % nz_dev
-                codes[h, z] = encode(ends[h, pl.ds(z * per_z, per_z), :], scale)
+                codes[h, z] = encode(ends[h, pl.ds(z * per_z, per_z), :], scale_of(z))
                 to = (z * ny_dev + me_y, me_m)
 
                 @pl.when(j < nz_dev - 1)
                 def _():
                     remote(codes.at[h, z], into.at[h, me_z], sem.at[h], sem.at[2 + h], to).start()
-                    remote(
-                        unit.at[h], units.at[h, me_z], scale_sem.at[unit_sem + h], scale_sem.at[unit_sem + 2 + h], to
-                    ).start()
+                    if with_unit:
+                        remote(
+                            es_send.at[h], es_recv.at[h, me_z], scale_sem.at[2 + h], scale_sem.at[4 + h], to
+                        ).start()
 
                 @pl.when(j == nz_dev - 1)
                 def _():
                     pltpu.make_async_copy(codes.at[h, z], into.at[h, me_z], sem.at[2 + h]).start()
-                    pltpu.make_async_copy(unit.at[h], units.at[h, me_z], scale_sem.at[unit_sem + 2 + h]).start()
+                    if with_unit:
+                        pltpu.make_async_copy(es_send.at[h], es_recv.at[h, me_z], scale_sem.at[4 + h]).start()
 
                 return carry
 
@@ -401,7 +402,8 @@
                 largest = jnp.maximum(largest, jnp.abs(values[y]))
             largest = jnp.max(largest, axis=0, keepdims=True)
             es_send[h] = largest * (1.0 / TOP)
-            send_ring(h, TOP / largest, e_send, e_recv, e_sem, es_send, es_recv, 2)
+            scale = TOP / largest
+            send_ring(h, lambda z: scale, e_send, e_recv, e_sem, True)
 
         def sweep_y(h):
             def one(x, carry):
@@ -414,32 +416,34 @@
             lax.fori_loop(0, XLO, one, 0)
 
         def scan_ring(h):
-            largest = jnp.full((8, BLOCK), 1e-30, F32)
             leap = fac[0, h] * fac[0, h]
             leap = leap * leap
             f = fwd[0, h]
+
+            def exclusive(given):
+                ordered = [jnp.where(f, given[s], given[nz_dev - 1 - s]) for s in range(nz_dev)]
+                taken = [jnp.zeros_like(ordered[0])]
+                for s in range(nz_dev - 1):
+                    taken.append(leap * taken[-1] + ordered[s])
+                return [jnp.where(f, taken[z], taken[nz_dev - 1 - z]) for z in range(nz_dev)]
+
+            bounds = exclusive([jnp.broadcast_to(es_recv[h, z], (8, BLOCK)) for z in range(nz_dev)])
+            for z in range(nz_dev):
+                bound[h, z] = bounds[z][:1]
             for part in range(per_z // 16):
                 got = [
                     decode(e_recv[h, z, part * 16 : part * 16 + 16, :]) * es_recv[h, z] for z in range(nz_dev)
                 ]
                 for i in range(2):
-                    given = [g[i * 8 : i * 8 + 8] for g in got]
-                    ordered = [jnp.where(f, given[s], given[nz_dev - 1 - s]) for s in range(nz_dev)]
-                    taken = [jnp.zeros_like(ordered[0])]
-                    for s in range(nz_dev - 1):
-                        taken.append(leap * taken[-1] + ordered[s])
+                    taken = exclusive([g[i * 8 : i * 8 + 8] for g in got])
                     for z in range(nz_dev):
-                        value = jnp.where(f, taken[z], taken[nz_dev - 1 - z])
                         start = z * per_z + part * 16 + i * 8
-                        ends[h, start : start + 8, :] = value
-                        largest = jnp.maximum(largest, jnp.abs(value))
-            largest = jnp.max(largest, axis=0, keepdims=True)
-            bs_send[h] = largest * (1.0 / TOP)
-            send_ring(h, TOP / largest, b_send, b_recv, b_sem, bs_send, bs_recv, 6)
+                        ends[h, start : start + 8, :] = taken[z]
+            send_ring(h, lambda z: 1.0 / jnp.maximum(bound[h, z], 1e-36), b_send, b_recv, b_sem, False)
 
         def finish_half(h):
             def inflow(z, carry):
-                ends[h, pl.ds(z * per_z, per_z), :] = decode(b_recv[h, z]) * bs_recv[h, z]
+                ends[h, pl.ds(z * per_z, per_z), :] = decode(b_recv[h, z]) * bound[h, me_z]
                 return carry
 
             lax.fori_loop(0, nz_dev, inflow, 0)
@@ -504,7 +508,6 @@
                 sweep_y(1)
         for h in range(2):
             await_bytes(b_recv.at[h], b_sem.at[2 + h])
-            await_bytes(bs_recv.at[h], scale_sem.at[8 + h])
             finish_half(h)
         await_bytes(xs_recv.at[pl.ds(0, group - 1)], scale_sem.at[0])
         for h in range(2):
@@ -512,7 +515,6 @@
             await_bytes(e_send.at[h, pl.ds(0, nz_dev - 1)], e_sem.at[h])
             await_bytes(es_recv.at[h, pl.ds(0, nz_dev - 1)], scale_sem.at[2 + h])
             await_bytes(b_send.at[h, pl.ds(0, nz_dev - 1)], b_sem.at[h])
-            await_bytes(bs_recv.at[h, pl.ds(0, nz_dev - 1)], scale_sem.at[6 + h])
         if not last:
             for h in range(2):
                 await_bytes(cur_b.at[h], c_sem.at[2 + h])
@@ -584,7 +586,6 @@
             pltpu.VMEM((2, nz_dev, 1, BLOCK), F32),
             pltpu.VMEM((2, nz_dev, per_z, BLOCK), I16),
             pltpu.VMEM((2, nz_dev, per_z, BLOCK), I16),
-            pltpu.VMEM((2, 1, BLOCK), F32),
             pltpu.VMEM((2, nz_dev, 1, BLOCK), F32),
             pltpu.VMEM((2, group, YLO * ZLO, BLOCK), BF16),
             pltpu.VMEM((2, ny_dev, tall, BLOCK), BF16),
@@ -602,7 +603,7 @@
             dma((4,)),
             dma((4,)),
             dma((4,)),
-            dma((10,)),
+            dma((6,)),
         ],
         compiler_params=pltpu.CompilerParams(
             collective_id=0, has_side_effects=True, vmem_limit_bytes=60 * 1024 * 1024

time: 98.3 us -> 96.4 us (0.981)
  Pallas kernels: 95.5 us -> 93.6 us
    pallas_call x1, Pallas kernels: 95.5 us -> 93.6 us  [local(): pl.pallas_call(functools.partial(kernel, dims), out_shape=jax.ShapeDtypeS...]
where the time goes in v6:
time: 96.4 us; the launch traced here: 95.5 us
  Pallas kernels  93.6 us (97%)
  local copies, waits for them, and re-layouts  1.87 us (2%)
    pallas_call x1, Pallas kernels, local(): pl.pallas_call(functools.partial(kernel, dims), out_shape=jax.ShapeDtypeS...  93.6 us

profile of v6, /device:TPU:6, one launch (start us, length us, event | category | flops | bytes accessed | tf_op | source)
XLA Modules:
  0.0 95.5 jit_solution(8361558225825261035)
XLA Ops:
  0.0 93.6 %shard_map.64 = bf16[256,1024]{1,0:T(8,128)(2,1)} custom-call(bf16[256,1024]{1,0:T(8,128)(2,1)} %bitcast.6, bf16[256,1024]{1,0:T(8,128)(2,1)} %bitcast.7, bf16[8,128,128]{2,1,0:T(8,128)(2,1)} %bitcast.8, s32[4,16]{1,0:T(4,128)} %bitcast.9, f32[3,256]{1,0:T(4,128)} %transmission_in.1, s32[3,256]{1,0:T(4,128)} %direction_in.1), custom_call_target="tpu_custom_call" | custom-call | flops 600000000 | bytes 2000000 | tf_op jit(solution)/shard_map/pallas_call | solution.py:555
  93.6 1.9 %copy.8 = bf16[256,1,1024]{2,0,1:T(8,128)(2,1)} copy(bf16[256,1,1024]{2,0,1:T(8,128)(2,1)} %bitcast.5) | data formatting | bytes 1048576

commit v7 on v6

--- a/solution.py
+++ b/solution.py
@@ -78,6 +78,7 @@
     coef_own,
     coef,
     work,
+    xscale,
     x_send,
     x_recv,
     xs_send,
@@ -199,19 +200,19 @@
             ]
             turned[m, h] = jnp.concatenate(rows, axis=0).astype(BF16)
 
-    def sweep_z(factor, forward):
-        values = run([work[pl.ds(z, 8, stride=nz), :] for z in range(nz)], factor, forward)
+    def sweep_z(m, factor, forward):
+        values = run([work[m, pl.ds(z, 8, stride=nz), :] for z in range(nz)], factor, forward)
         largest = jnp.abs(values[0])
         for z in range(nz):
-            work[pl.ds(z, 8, stride=nz), :] = values[z]
+            work[m, pl.ds(z, 8, stride=nz), :] = values[z]
             if z:
                 largest = jnp.maximum(largest, jnp.abs(values[z]))
         largest = jnp.maximum(jnp.max(largest, axis=0, keepdims=True), 1e-30)
         return TOP / largest, largest * (1.0 / TOP)
 
-    def two_rows(h, y, zh):
+    def two_rows(m, h, y, zh):
         start = h * chunk + y * nz + zh * ZLO
-        return jnp.concatenate([work[start : start + ZLO, :], work[start + nz : start + nz + ZLO, :]], axis=0)
+        return jnp.concatenate([work[m, start : start + ZLO, :], work[m, start + nz : start + nz + ZLO, :]], axis=0)
 
     loads[1].wait()
     pl.semaphore_wait(barrier, len(near))
@@ -257,14 +258,14 @@
     def sweep_source(m, carry):
         for h in range(2):
             columns = pl.ds(pl.multiple_of(m * chunk, chunk), chunk)
-            work[h * chunk : (h + 1) * chunk, :] = nt(eye, source_v[h * BLOCK : (h + 1) * BLOCK, columns])
-        scale, unit = sweep_z(coef_own[0], coef_own[1] > 0.5)
+            work[m, h * chunk : (h + 1) * chunk, :] = nt(eye, source_v[h * BLOCK : (h + 1) * BLOCK, columns])
+        scale, unit = sweep_z(m, coef_own[0], coef_own[1] > 0.5)
         ss_send[m] = unit
         for zh in range(ny_dev):
             for h in range(2):
                 for y in range(0, YLO, 2):
                     rows = pl.ds(m * YLO * ZLO + y * ZLO, 2 * ZLO)
-                    s_send[zh, h, rows, :] = encode(two_rows(h, y, zh), scale)
+                    s_send[zh, h, rows, :] = encode(two_rows(m, h, y, zh), scale)
         return carry
 
     lax.fori_loop(0, nm, sweep_source, 0)
@@ -302,15 +303,13 @@
                 total = nt(left, right)
                 for zh in range(ny_dev):
                     for y in range(YLO):
-                        work[h * chunk + y * nz + zh * ZLO : h * chunk + y * nz + (zh + 1) * ZLO, :] = total[
+                        work[m, h * chunk + y * nz + zh * ZLO : h * chunk + y * nz + (zh + 1) * ZLO, :] = total[
                             (zh * YLO + y) * ZLO : (zh * YLO + y + 1) * ZLO
                         ]
-            scale, unit = sweep_z(coef[m, 0], coef[m, 1] > 0.5)
+            scale, unit = sweep_z(m, coef[m, 0], coef[m, 1] > 0.5)
             xs_send[m] = unit
-            for zh in range(ny_dev):
-                for h in range(2):
-                    for y in range(0, YLO, 2):
-                        x_send[h, m * ny_dev + zh, y * ZLO : (y + 2) * ZLO, :] = encode(two_rows(h, y, zh), scale)
+            xscale[m] = scale
+            code(m, 0)
             send_codes(j, 0, True)
             return carry
 
@@ -339,7 +338,14 @@
                     pl.when(j < nm - 1)(send)
                     pl.when(j == nm - 1)(keep)
 
+        def code(m, h):
+            for zh in range(ny_dev):
+                for y in range(0, YLO, 2):
+                    rows = two_rows(m, h, y, zh)
+                    x_send[h, m * ny_dev + zh, y * ZLO : (y + 2) * ZLO, :] = encode(rows, xscale[m])
+
         def send_second(j, carry):
+            code(mode_at(j), 1)
             send_codes(j, 1, False)
             return carry
 
@@ -573,7 +579,8 @@
             pltpu.VMEM((nm, 2 * PER_ROW, BLOCK, BLOCK), BF16),
             pltpu.VMEM((2, 8, BLOCK), F32),
             pltpu.VMEM((nm, 2, 8, BLOCK), F32),
-            pltpu.VMEM((2 * chunk, BLOCK), F32),
+            pltpu.VMEM((nm, 2 * chunk, BLOCK), F32),
+            pltpu.VMEM((nm, 1, BLOCK), F32),
             pltpu.VMEM((2, group, YLO * ZLO, BLOCK), I16),
             pltpu.VMEM((2, group, YLO * ZLO, BLOCK), I16),
             pltpu.VMEM((nm, 1, BLOCK), F32),

time: 96.4 us -> 96.3 us (level)
  no operation moved by 1% of the time
where the time goes in v7:
time: 96.3 us; the launch traced here: 95.2 us
  Pallas kernels  93.4 us (97%)
  local copies, waits for them, and re-layouts  1.87 us (2%)
    pallas_call x1, Pallas kernels, local(): pl.pallas_call(functools.partial(kernel, dims), out_shape=jax.ShapeDtypeS...  93.4 us

profile of v7, /device:TPU:6, one launch (start us, length us, event | category | flops | bytes accessed | tf_op | source)
XLA Modules:
  0.0 95.2 jit_solution(7025734794812436308)
XLA Ops:
  0.0 93.4 %shard_map.64 = bf16[256,1024]{1,0:T(8,128)(2,1)} custom-call(bf16[256,1024]{1,0:T(8,128)(2,1)} %bitcast.6, bf16[256,1024]{1,0:T(8,128)(2,1)} %bitcast.7, bf16[8,128,128]{2,1,0:T(8,128)(2,1)} %bitcast.8, s32[4,16]{1,0:T(4,128)} %bitcast.9, f32[3,256]{1,0:T(4,128)} %transmission_in.1, s32[3,256]{1,0:T(4,128)} %direction_in.1), custom_call_target="tpu_custom_call" | custom-call | flops 600000000 | bytes 2000000 | tf_op jit(solution)/shard_map/pallas_call | solution.py:561
  93.4 1.9 %copy.8 = bf16[256,1,1024]{2,0,1:T(8,128)(2,1)} copy(bf16[256,1,1024]{2,0,1:T(8,128)(2,1)} %bitcast.5) | data formatting | bytes 1048576
